TPU v7x, 256 devices: a whole 4x4x8 slice. The times are simulated.
256 devices in a mesh: seq: 64 (over z, x, core), dp: 4 (over y).
Axes of the slice: x: 4, y: 4, z: 8, core: 2. Of those that a mesh axis runs over, the one named last changes fastest.
Arguments:
- qkv: bfloat16 [4, 16384, 3, 512], P('dp', 'seq'), may hold values from -16 to 16
- dout: bfloat16 [4, 16384, 1024], P('dp', 'seq'), may hold values from -6 to 6
- out_weight: bfloat16 [512, 1024], replicated, may hold values from -0.25 to 0.25
- head_offsets: int32 [2, 8], replicated, may hold values from 0 to 15, as said below
Outputs:
- grad_qkv: bfloat16 [4, 16384, 3, 512], P('dp', 'seq')
- weight_grad: float32 [512, 1024], P('seq')
Inputs may be any that keep to these rules, and one draw needn't show every extreme that they name: `head_offsets`: row 0 holds values below 4, row 1 values below 16; each row holds 0 and its largest allowed value.
All inputs are finite; a program needn't handle non-finite values.
Results may differ from a plain program's by a relative error of at most 0.02.
Values may be sent and summed in bfloat16 or wider, within the bound.
A program may use at most 64 MiB of HBM per device.

v0:
```python
import jax
import jax.numpy as jnp
from jax import lax
from jax.sharding import PartitionSpec as P

H = 8
E = 64
W1 = 256
R2 = 4
R3 = 16
GROUP2 = 4


def partner(block, axis, distance):
    count = lax.axis_size(axis)
    route = []
    for low in range(count):
        high = low | 1 << distance
        if high != low and high < count:
            route += [(low, high), (high, low)]
    return lax.ppermute(block, axis, route)


def residue_mask(dilation, offsets_row):
    return jnp.arange(dilation)[:, None] == offsets_row[None, :]


def select_rows(array, dilation, offsets_row):
    shaped = array.reshape(array.shape[0] // dilation, dilation, H * E)
    column_mask = jnp.repeat(residue_mask(dilation, offsets_row), E, axis=1)
    return jnp.sum(jnp.where(column_mask[None], shaped, jnp.zeros_like(shaped)), axis=1)


def select_stats(array, dilation, offsets_row):
    shaped = array.reshape(array.shape[0] // dilation, dilation, H)
    head_mask = residue_mask(dilation, offsets_row)
    return jnp.sum(jnp.where(head_mask[None], shaped, jnp.zeros_like(shaped)), axis=1)


def place_rows(array, dilation, offsets_row):
    column_mask = jnp.repeat(residue_mask(dilation, offsets_row), E, axis=1)
    widened = jnp.where(column_mask[None], array[:, None, :], 0.0)
    return widened.reshape(array.shape[0] * dilation, H * E)


def place_stats(array, dilation, offsets_row, filler):
    head_mask = residue_mask(dilation, offsets_row)
    widened = jnp.where(head_mask[None], array[:, None, :], jnp.asarray(filler, array.dtype))
    return widened.reshape(array.shape[0] * dilation, H)


def head_pair(array, first_head):
    columns = array[:, :, first_head * E : (first_head + 2) * E]
    return columns.reshape(array.shape[0], array.shape[1], 2, E)


def forward_block(query_rows, key_rows, value_rows):
    score_scale = E ** (-0.5)
    maxima, totals, weighted_parts = ([], [], [])
    for first_head in range(0, H, 2):
        query_pair = head_pair(query_rows, first_head)
        key_pair = head_pair(key_rows, first_head)
        value_pair = head_pair(value_rows, first_head)
        scores = (
            jnp.einsum("sqhe,skhe->shqk", query_pair, key_pair, preferred_element_type=jnp.float32)
            * score_scale
        )
        row_max = jnp.max(scores, axis=3)
        weights = jnp.exp(scores - row_max[..., None])
        totals.append(jnp.swapaxes(jnp.sum(weights, axis=3), 1, 2))
        maxima.append(jnp.swapaxes(row_max, 1, 2))
        weighted = jnp.einsum(
            "shqk,skhe->sqhe",
            weights.astype(jnp.bfloat16),
            value_pair,
            preferred_element_type=jnp.float32,
        )
        weighted_parts.append(weighted.reshape(query_rows.shape[0], query_rows.shape[1], 2 * E))
    return (
        jnp.concatenate(maxima, 2),
        jnp.concatenate(totals, 2),
        jnp.concatenate(weighted_parts, 2),
    )


def backward_block(query_rows, key_rows, value_rows, grad_rows, log_totals, grad_dots):
    score_scale = E ** (-0.5)
    query_grads, key_grads, value_grads = ([], [], [])
    for first_head in range(0, H, 2):
        query_pair = head_pair(query_rows, first_head)
        key_pair = head_pair(key_rows, first_head)
        value_pair = head_pair(value_rows, first_head)
        grad_pair = head_pair(grad_rows, first_head)
        log_pair = jnp.swapaxes(log_totals[:, :, first_head : first_head + 2], 1, 2)[..., None]
        dots_pair = jnp.swapaxes(grad_dots[:, :, first_head : first_head + 2], 1, 2)[..., None]
        scores = (
            jnp.einsum("sqhe,skhe->shqk", query_pair, key_pair, preferred_element_type=jnp.float32)
            * score_scale
        )
        probabilities = jnp.exp(scores - log_pair)
        grad_probs = jnp.einsum(
            "sqhe,skhe->shqk", grad_pair, value_pair, preferred_element_type=jnp.float32
        )
        grad_scores = probabilities * (grad_probs - dots_pair)
        probs_low = probabilities.astype(jnp.bfloat16)
        scores_low = grad_scores.astype(jnp.bfloat16)
        grad_values = jnp.einsum(
            "shqk,sqhe->skhe", probs_low, grad_pair, preferred_element_type=jnp.float32
        )
        grad_queries = (
            jnp.einsum("shqk,skhe->sqhe", scores_low, key_pair, preferred_element_type=jnp.float32)
            * score_scale
        )
        grad_keys = (
            jnp.einsum(
                "shqk,sqhe->skhe", scores_low, query_pair, preferred_element_type=jnp.float32
            )
            * score_scale
        )
        query_grads.append(grad_queries.reshape(query_rows.shape[0], query_rows.shape[1], 2 * E))
        key_grads.append(grad_keys.reshape(key_rows.shape[0], key_rows.shape[1], 2 * E))
        value_grads.append(grad_values.reshape(key_rows.shape[0], key_rows.shape[1], 2 * E))
    return (
        jnp.concatenate(query_grads, 2),
        jnp.concatenate(key_grads, 2),
        jnp.concatenate(value_grads, 2),
    )


def doubling(blocks, bit_count, sender, position):
    for bit_index in range(bit_count):
        arrived = sender(blocks, bit_index)
        upper = position >> bit_index & 1 == 1
        blocks = jnp.where(
            upper,
            jnp.concatenate([arrived, blocks], axis=1),
            jnp.concatenate([blocks, arrived], axis=1),
        )
    return blocks


def halving(blocks, bit_count, sender, position):
    for bit_index in reversed(range(bit_count)):
        half_rows = blocks.shape[1] // 2
        lower_part = blocks[:, :half_rows]
        upper_part = blocks[:, half_rows:]
        upper = position >> bit_index & 1 == 1
        kept_part = jnp.where(upper, upper_part, lower_part)
        sent_part = jnp.where(upper, lower_part, upper_part)
        blocks = kept_part + sender(sent_part, bit_index)
    return blocks


def sparse_forward(query_sparse, pair_all, dilation, offsets_row):
    row_max, row_total, weighted = forward_block(
        query_sparse[None], pair_all[0][None], pair_all[1][None]
    )
    dense_max = place_stats(row_max[0], dilation, offsets_row, -jnp.inf)
    dense_total = place_stats(row_total[0], dilation, offsets_row, 0.0)
    dense_weighted = place_rows(weighted[0], dilation, offsets_row)
    return (dense_max, dense_total, dense_weighted)


def local(qkv, dout, out_weight, head_offsets):
    tokens_here = qkv.shape[1]
    attn_width = H * E
    query_rows = qkv[0, :, 0]
    key_rows = qkv[0, :, 1]
    value_rows = qkv[0, :, 2]
    grads_in = dout[0]
    position = lax.axis_index("seq")
    seq_count = lax.axis_size("seq")
    group_far = min(16, seq_count)
    bits_far = group_far.bit_length() - 1
    bits_near = GROUP2.bit_length() - 1
    near_offsets = head_offsets[0]
    far_offsets = head_offsets[1]
    near_query = select_rows(query_rows, R2, near_offsets)
    near_pair = jnp.stack(
        [select_rows(key_rows, R2, near_offsets), select_rows(value_rows, R2, near_offsets)]
    )
    far_query = select_rows(query_rows, R3, far_offsets)
    far_pair = jnp.stack(
        [select_rows(key_rows, R3, far_offsets), select_rows(value_rows, R3, far_offsets)]
    )
    near_all = doubling(
        near_pair,
        bits_near,
        lambda outgoing, bit_index: partner(outgoing, "seq", bit_index),
        position,
    )
    far_all = doubling(
        far_pair,
        bits_far,
        lambda outgoing, bit_index: partner(outgoing, "seq", bit_index),
        position,
    )
    local_count = tokens_here // W1
    local_query = query_rows.reshape(local_count, W1, attn_width)
    local_key = key_rows.reshape(local_count, W1, attn_width)
    local_value = value_rows.reshape(local_count, W1, attn_width)
    max_one, total_one, weighted_one = forward_block(local_query, local_key, local_value)
    max_one = max_one.reshape(tokens_here, H)
    total_one = total_one.reshape(tokens_here, H)
    weighted_one = weighted_one.reshape(tokens_here, attn_width)
    max_two, total_two, weighted_two = sparse_forward(near_query, near_all, R2, near_offsets)
    max_three, total_three, weighted_three = sparse_forward(far_query, far_all, R3, far_offsets)
    row_peak = jnp.maximum(jnp.maximum(max_one, max_two), max_three)
    factor_one = jnp.exp(max_one - row_peak)
    factor_two = jnp.exp(max_two - row_peak)
    factor_three = jnp.exp(max_three - row_peak)
    row_denom = factor_one * total_one + factor_two * total_two + factor_three * total_three
    blended = (
        factor_one[:, :, None] * weighted_one.reshape(tokens_here, H, E)
        + factor_two[:, :, None] * weighted_two.reshape(tokens_here, H, E)
        + factor_three[:, :, None] * weighted_three.reshape(tokens_here, H, E)
    )
    combined = blended / row_denom[:, :, None]
    log_totals = row_peak + jnp.log(row_denom)
    attention = combined.reshape(tokens_here, attn_width).astype(jnp.bfloat16)
    grad_attn = lax.dot_general(
        grads_in, out_weight, (((1,), (1,)), ((), ())), preferred_element_type=jnp.float32
    ).astype(jnp.bfloat16)
    grad_dots = jnp.sum(
        (grad_attn.astype(jnp.float32) * attention.astype(jnp.float32)).reshape(tokens_here, H, E),
        axis=2,
    )
    rows_here = attn_width // seq_count
    weight_local = lax.dot_general(
        attention, grads_in, (((0,), (0,)), ((), ())), preferred_element_type=jnp.float32
    )
    weight_summed = lax.psum(weight_local, ("seq", "dp"))
    weight_grad = lax.dynamic_slice_in_dim(weight_summed, position * rows_here, rows_here, 0)
    weight_grad = weight_grad / lax.axis_size("dp")
    grad_q_one, grad_k_one, grad_v_one = backward_block(
        local_query,
        local_key,
        local_value,
        grad_attn.reshape(local_count, W1, attn_width),
        log_totals.reshape(local_count, W1, H),
        grad_dots.reshape(local_count, W1, H),
    )
    near_grads = select_rows(grad_attn, R2, near_offsets)
    near_stack = jnp.stack(
        [select_stats(log_totals, R2, near_offsets), select_stats(grad_dots, R2, near_offsets)]
    )
    grad_q_two, grad_k_near, grad_v_near = backward_block(
        near_query[None],
        near_all[0][None],
        near_all[1][None],
        near_grads[None],
        near_stack[0][None],
        near_stack[1][None],
    )
    far_grads = select_rows(grad_attn, R3, far_offsets)
    far_stack = jnp.stack(
        [select_stats(log_totals, R3, far_offsets), select_stats(grad_dots, R3, far_offsets)]
    )
    grad_q_three, grad_k_far, grad_v_far = backward_block(
        far_query[None],
        far_all[0][None],
        far_all[1][None],
        far_grads[None],
        far_stack[0][None],
        far_stack[1][None],
    )
    near_back = halving(
        jnp.stack([grad_k_near[0], grad_v_near[0]]),
        bits_near,
        lambda outgoing, bit_index: partner(outgoing.astype(jnp.bfloat16), "seq", bit_index).astype(
            outgoing.dtype
        ),
        position,
    )
    far_back = halving(
        jnp.stack([grad_k_far[0], grad_v_far[0]]),
        bits_far,
        lambda outgoing, bit_index: partner(outgoing.astype(jnp.bfloat16), "seq", bit_index).astype(
            outgoing.dtype
        ),
        position,
    )
    grad_queries = (
        grad_q_one.reshape(tokens_here, attn_width)
        + place_rows(grad_q_two[0], R2, near_offsets)
        + place_rows(grad_q_three[0], R3, far_offsets)
    )
    grad_keys = (
        grad_k_one.reshape(tokens_here, attn_width)
        + place_rows(near_back[0], R2, near_offsets)
        + place_rows(far_back[0], R3, far_offsets)
    )
    grad_values = (
        grad_v_one.reshape(tokens_here, attn_width)
        + place_rows(near_back[1], R2, near_offsets)
        + place_rows(far_back[1], R3, far_offsets)
    )
    grad_qkv = jnp.stack([grad_queries, grad_keys, grad_values], axis=1).astype(jnp.bfloat16)[None]
    return (grad_qkv, weight_grad)


def solution(mesh):
    return jax.shard_map(
        local,
        mesh=mesh,
        in_specs=(P("dp", "seq", None, None), P("dp", "seq", None), P(), P()),
        out_specs=(P("dp", "seq", None, None), P("seq", None)),
        check_vma=False,
    )
```

profile of v0, /device:TPU:1, one launch (start us, length us, event | category | flops | bytes accessed | tf_op | source)
XLA Modules:
  0.0 604.6 jit_solution(375854798139022955)
XLA Ops:
  7.2 2.1 slice_bitcast_fusion.30
  12.9 2.1 select_reduce_fusion.6
  15.7 3.2 collective-permute-start
  30.0 1.7 fusion.68
  35.6 2.6 collective-permute-done.3
  40.8 1.9 maximum_select_fusion.2
  56.4 1.7 copy.415
  58.0 1.7 copy.414
  59.7 1.6 copy.413
  80.1 1.9 pad_maximum_fusion.1
  82.0 2.0 copy.533
  84.1 1.9 maximum_select_fusion.3
  85.9 1.7 collective-permute-start.5
  98.3 1.7 fusion.111
  103.4 1.7 fusion.113
  108.5 1.7 fusion.115
  114.7 1.7 maximum_bitcast_fusion.3
  116.4 1.7 copy.423
  118.1 1.8 broadcast_select_fusion.7
  121.2 2.0 select_n.528
  123.3 2.4 select_n.573
  136.2 2.3 copy.534
  165.7 2.1 copy.437
  169.3 2.0 copy.433
  193.0 2.0 copy.424
  196.6 2.0 copy.417
  198.6 3.2 convert_multiply_fusion
  201.8 2.1 copy.438
  203.9 1.7 bitcast_reduce_fusion
  231.3 1.8 fusion.103
  242.9 1.6 convolution_multiply_fusion.25
  259.2 1.7 convolution_multiply_fusion.27
  263.9 1.7 fusion.146
  287.2 1.7 fusion.56
  304.8 1.7 copy.527
  314.2 1.7 copy.504
  315.9 1.7 copy.503
  317.6 1.7 copy.502
  319.2 1.6 copy.501
  320.9 1.7 copy.453
  324.2 1.7 copy.451
  327.5 2.3 copy.535
  331.4 1.8 fusion.41
  335.8 1.9 collective-permute-start.9
  338.8 3.4 collective-permute-start.7
  345.2 3.0 collective-permute-done.10
  349.3 5.2 collective-permute-start.11
  365.2 231.1 %all-reduce.2.cloned.1.call-done = f32[512,1024]{1,0:T(8,128)} async-done(((f32[512,1024]{1,0:T(8,128)}), f32[512,1024]{1,0:T(8,128)}) %all-reduce.2.cloned.1.call-update) | async-done | bytes 2097168 | tf_op jit(solution)/shard_map/psum | solution.py:232
  (472 shorter events, 262.2 us)
Async XLA Ops:
  7.2 589.2 %all-reduce.2.cloned.1.call-start = ((), (), s32[]{:S(2)}) async-start(), calls=%async_computation | async-start | bytes 4194304 | tf_op jit(solution)/shard_map/psum | solution.py:232
  12.8 8.9 %copy-start.64 = (bf16[16,512]{1,0:T(8,128)(2,1)}, bf16[16,512]{1,0:T(8,128)(2,1)S(1)}, u32[]{:S(2)}) copy-start(bf16[16,512]{1,0:T(8,128)(2,1)S(1)} %get-tuple-element.4) | copy-start | bytes 49156
  12.8 8.8 %copy-start.11 = (bf16[1,256,512]{2,1,0:T(8,128)(2,1)S(1)}, bf16[1,256,512]{2,1,0:T(8,128)(2,1)}, u32[]{:S(2)}) copy-start(bf16[1,256,512]{2,1,0:T(8,128)(2,1)} %get-tuple-element.18) | copy-start | bytes 786436
  12.8 8.8 %copy-start.12 = (bf16[1,256,512]{2,1,0:T(8,128)(2,1)S(1)}, bf16[1,256,512]{2,1,0:T(8,128)(2,1)}, u32[]{:S(2)}) copy-start(bf16[1,256,512]{2,1,0:T(8,128)(2,1)} %get-tuple-element.20) | copy-start | bytes 786436
  15.0 6.5 %copy-start.42 = (bf16[64,512]{1,0:T(8,128)(2,1)}, bf16[64,512]{1,0:T(8,128)(2,1)S(1)}, u32[]{:S(2)}) copy-start(bf16[64,512]{1,0:T(8,128)(2,1)S(1)} %get-tuple-element.8) | copy-start | bytes 196612
  15.0 6.7 %copy-start.43 = (bf16[64,512]{1,0:T(8,128)(2,1)}, bf16[64,512]{1,0:T(8,128)(2,1)S(1)}, u32[]{:S(2)}) copy-start(bf16[64,512]{1,0:T(8,128)(2,1)S(1)} %get-tuple-element.9) | copy-start | bytes 196612
  15.7 25.1 %collective-permute-start = (bf16[2,64,512]{2,1,0:T(8,128)(2,1)}, bf16[2,64,512]{2,1,0:T(8,128)(2,1)}, u32[]{:S(2)}, u32[]{:S(2)}) collective-permute-start(bf16[2,64,512]{2,1,0:T(8,128)(2,1)} %pad_maximum_fusion.2), channel_id=1, source_target_pairs={{0,4},{4,0},{8,12},{12,8},{16,20},{20,16},{24,28},{28,24},{32,36},... | collective-permute-start | bytes 393224 | tf_op jit(solution)/shard_map/ppermute | solution.py:21
  19.6 13.7 %collective-permute-start.2 = (bf16[2,16,512]{2,1,0:T(8,128)(2,1)}, bf16[2,16,512]{2,1,0:T(8,128)(2,1)}, u32[]{:S(2)}, u32[]{:S(2)}) collective-permute-start(bf16[2,16,512]{2,1,0:T(8,128)(2,1)} %pad_maximum_fusion.3), channel_id=1, source_target_pairs={{0,4},{4,0},{8,12},{12,8},{16,20},{20,16},{24,28},{28,24},{32,36},... | collective-permute-start | bytes 98312 | tf_op jit(solution)/shard_map/ppermute | solution.py:21
  22.3 7.1 %copy-start.17 = (bf16[1,256,128]{1,2,0:T(8,128)(2,1)}, bf16[1,256,128]{1,2,0:T(8,128)(2,1)S(1)}, u32[]{:S(2)}) copy-start(bf16[1,256,128]{1,2,0:T(8,128)(2,1)S(1)} %copy.370) | copy-start | bytes 196612
  22.4 7.0 %copy-start.19 = (bf16[1,256,128]{1,2,0:T(8,128)(2,1)}, bf16[1,256,128]{1,2,0:T(8,128)(2,1)S(1)}, u32[]{:S(2)}) copy-start(bf16[1,256,128]{1,2,0:T(8,128)(2,1)S(1)} %copy.371) | copy-start | bytes 196612
  22.5 7.2 %copy-start.13 = (bf16[1,256,128]{1,2,0:T(8,128)(2,1)}, bf16[1,256,128]{1,2,0:T(8,128)(2,1)S(1)}, u32[]{:S(2)}) copy-start(bf16[1,256,128]{1,2,0:T(8,128)(2,1)S(1)} %copy.368) | copy-start | bytes 196612
  22.6 7.1 %copy-start.15 = (bf16[1,256,128]{1,2,0:T(8,128)(2,1)}, bf16[1,256,128]{1,2,0:T(8,128)(2,1)S(1)}, u32[]{:S(2)}) copy-start(bf16[1,256,128]{1,2,0:T(8,128)(2,1)S(1)} %copy.369) | copy-start | bytes 196612
  23.1 5.7 copy-start.73
  30.0 25.6 %copy-start.59 = (f32[2,256,64]{1,2,0:T(8,128)S(1)}, f32[2,256,64]{1,2,0:T(8,128)}, u32[]{:S(2)}) copy-start(f32[2,256,64]{1,2,0:T(8,128)} %fusion.64) | copy-start | bytes 393220
  34.8 3.4 collective-permute-start.3
  35.6 15.0 %copy-start.81 = (f32[2,256]{1,0:T(2,128)}, f32[2,256]{1,0:T(2,128)S(1)}, u32[]{:S(2)}) copy-start(f32[2,256]{1,0:T(2,128)S(1)} %fusion.45) | copy-start | bytes 6148
  39.8 44.2 %collective-permute-start.4 = (bf16[2,64,512]{2,1,0:T(8,128)(2,1)}, bf16[2,64,512]{2,1,0:T(8,128)(2,1)}, u32[]{:S(2)}, u32[]{:S(2)}) collective-permute-start(bf16[2,64,512]{2,1,0:T(8,128)(2,1)} %maximum_select_fusion.4), channel_id=1, source_target_pairs={{0,16},{16,0},{4,20},{20,4},{8,24},{24,8},{12,28},{28,12},{32,48},... | collective-permute-start | bytes 393224 | tf_op jit(solution)/shard_map/ppermute | solution.py:21
  42.7 44.9 %collective-permute-start.1 = (bf16[2,128,512]{2,1,0:T(8,128)(2,1)}, bf16[2,128,512]{2,1,0:T(8,128)(2,1)}, u32[]{:S(2)}, u32[]{:S(2)}) collective-permute-start(bf16[2,128,512]{2,1,0:T(8,128)(2,1)} %maximum_select_fusion.2), channel_id=1, source_target_pairs={{0,8},{8,0},{4,12},{12,4},{16,24},{24,16},{20,28},{28,20},{32,40},... | collective-permute-start | bytes 786440 | tf_op jit(solution)/shard_map/ppermute | solution.py:21
  50.6 99.5 %copy-start.71 = (bf16[16,2,64]{2,1,0:T(2,128)(2,1)}, bf16[16,2,64]{2,1,0:T(2,128)(2,1)S(1)}, u32[]{:S(2)}) copy-start(bf16[16,2,64]{2,1,0:T(2,128)(2,1)S(1)} %reshape.1948) | copy-start | bytes 12292
  51.4 100.3 %copy-start.70 = (bf16[16,2,64]{2,1,0:T(2,128)(2,1)}, bf16[16,2,64]{2,1,0:T(2,128)(2,1)S(1)}, u32[]{:S(2)}) copy-start(bf16[16,2,64]{2,1,0:T(2,128)(2,1)S(1)} %reshape.1946) | copy-start | bytes 12292
  63.5 25.5 %copy-start.10 = (f32[1,256,8]{2,1,0:T(8,128)}, f32[1,256,8]{2,1,0:T(8,128)S(1)}, u32[]{:S(2)}) copy-start(f32[1,256,8]{2,1,0:T(8,128)S(1)} %copy.460) | copy-start | bytes 24580
  85.9 52.6 %collective-permute-start.5 = (bf16[2,128,512]{2,1,0:T(8,128)(2,1)}, bf16[2,128,512]{2,1,0:T(8,128)(2,1)}, u32[]{:S(2)}, u32[]{:S(2)}) collective-permute-start(bf16[2,128,512]{2,1,0:T(8,128)(2,1)} %maximum_select_fusion.3), channel_id=1, source_target_pairs={{0,32},{32,0},{4,36},{36,4},{8,40},{40,8},{12,44},{44,12},{16,48},... | collective-permute-start | bytes 786440 | tf_op jit(solution)/shard_map/ppermute | solution.py:21
  93.8 17.9 %copy-start.41 = (bf16[1,256,128]{1,2,0:T(8,128)(2,1)}, bf16[1,256,128]{1,2,0:T(8,128)(2,1)S(1)}, u32[]{:S(2)}) copy-start(bf16[1,256,128]{1,2,0:T(8,128)(2,1)S(1)} %copy.380) | copy-start | bytes 196612
  94.8 16.9 %copy-start.40 = (bf16[1,256,128]{1,2,0:T(8,128)(2,1)}, bf16[1,256,128]{1,2,0:T(8,128)(2,1)S(1)}, u32[]{:S(2)}) copy-start(bf16[1,256,128]{1,2,0:T(8,128)(2,1)S(1)} %copy.378) | copy-start | bytes 196612
  159.0 5.9 copy-start.67
  165.7 24.9 %copy-start.66 = (pred[16,512]{1,0:T(8,128)(4,1)S(1)}, pred[16,512]{1,0:T(8,128)(4,1)}, u32[]{:S(2)}) copy-start(pred[16,512]{1,0:T(8,128)(4,1)} %copy-done.65) | copy-start | bytes 24580
  201.8 38.4 %copy-start.5 = (f32[2,64,256]{2,1,0:T(8,128)S(1)}, f32[2,64,256]{2,1,0:T(8,128)}, u32[]{:S(2)}) copy-start(f32[2,64,256]{2,1,0:T(8,128)} %copy-done.4) | copy-start | bytes 393220
  205.6 43.4 %copy-start.3 = (f32[2,64,256]{2,1,0:T(8,128)S(1)}, f32[2,64,256]{2,1,0:T(8,128)}, u32[]{:S(2)}) copy-start(f32[2,64,256]{2,1,0:T(8,128)} %copy-done.2) | copy-start | bytes 393220
  242.9 19.5 %copy-start.7 = (f32[64,4,8]{2,1,0:T(4,128)S(1)}, f32[64,4,8]{2,1,0:T(4,128)}, u32[]{:S(2)}) copy-start(f32[64,4,8]{2,1,0:T(4,128)} %copy.397) | copy-start | bytes 24580
  259.2 14.7 %copy-start.72 = (bf16[16,2,64]{2,1,0:T(2,128)(2,1)S(1)}, bf16[16,2,64]{2,1,0:T(2,128)(2,1)}, u32[]{:S(2)}) copy-start(bf16[16,2,64]{2,1,0:T(2,128)(2,1)} %reshape.1950) | copy-start | bytes 12292
  259.2 15.6 %copy-start.58 = (f32[2,16,256]{2,1,0:T(8,128)S(1)}, f32[2,16,256]{2,1,0:T(8,128)}, u32[]{:S(2)}) copy-start(f32[2,16,256]{2,1,0:T(8,128)} %get-tuple-element.120) | copy-start | bytes 98308
  259.2 15.6 %copy-start.83 = (bf16[16,2,64]{2,1,0:T(2,128)(2,1)S(1)}, bf16[16,2,64]{2,1,0:T(2,128)(2,1)}, u32[]{:S(2)}) copy-start(bf16[16,2,64]{2,1,0:T(2,128)(2,1)} %reshape.2010) | copy-start | bytes 12292
  259.2 29.7 %copy-start.35 = (bf16[1,256,128]{1,2,0:T(8,128)(2,1)S(1)}, bf16[1,256,128]{1,2,0:T(8,128)(2,1)}, u32[]{:S(2)}) copy-start(bf16[1,256,128]{1,2,0:T(8,128)(2,1)} %copy-done.34) | copy-start | bytes 196612
  259.2 29.7 %copy-start.39 = (bf16[1,256,128]{1,2,0:T(8,128)(2,1)S(1)}, bf16[1,256,128]{1,2,0:T(8,128)(2,1)}, u32[]{:S(2)}) copy-start(bf16[1,256,128]{1,2,0:T(8,128)(2,1)} %copy.447) | copy-start | bytes 196612
  263.7 25.5 %copy-start.22 = (bf16[1,256,128]{1,2,0:T(8,128)(2,1)S(1)}, bf16[1,256,128]{1,2,0:T(8,128)(2,1)}, u32[]{:S(2)}) copy-start(bf16[1,256,128]{1,2,0:T(8,128)(2,1)} %copy-done.21) | copy-start | bytes 196612
  266.5 23.6 %copy-start.28 = (bf16[1,256,128]{1,2,0:T(8,128)(2,1)S(1)}, bf16[1,256,128]{1,2,0:T(8,128)(2,1)}, u32[]{:S(2)}) copy-start(bf16[1,256,128]{1,2,0:T(8,128)(2,1)} %copy-done.27) | copy-start | bytes 196612
  271.3 19.6 %copy-start.38 = (bf16[1,256,128]{1,2,0:T(8,128)(2,1)S(1)}, bf16[1,256,128]{1,2,0:T(8,128)(2,1)}, u32[]{:S(2)}) copy-start(bf16[1,256,128]{1,2,0:T(8,128)(2,1)} %copy.444) | copy-start | bytes 196612
  276.6 15.2 %copy-start.33 = (bf16[1,256,128]{1,2,0:T(8,128)(2,1)S(1)}, bf16[1,256,128]{1,2,0:T(8,128)(2,1)}, u32[]{:S(2)}) copy-start(bf16[1,256,128]{1,2,0:T(8,128)(2,1)} %copy-done.32) | copy-start | bytes 196612
  303.4 34.3 %collective-permute-start.6 = (bf16[2,128,512]{1,2,0:T(8,128)(2,1)}, bf16[2,128,512]{1,2,0:T(8,128)(2,1)}, u32[]{:S(2)}, u32[]{:S(2)}) collective-permute-start(bf16[2,128,512]{1,2,0:T(8,128)(2,1)} %select_convert_fusion.5), channel_id=1, source_target_pairs={{0,8},{8,0},{4,12},{12,4},{16,24},{24,16},{20,28},{28,20},{32,40},... | collective-permute-start | bytes 786440 | tf_op jit(solution)/shard_map/ppermute | solution.py:21
  313.5 16.3 %copy-start.69 = (f32[256,8]{0,1:T(8,128)S(1)}, f32[256,8]{0,1:T(8,128)}, u32[]{:S(2)}) copy-start(f32[256,8]{0,1:T(8,128)} %copy-done.68) | copy-start | bytes 24580
  314.2 20.4 %collective-permute-start.8 = (bf16[2,128,512]{1,2,0:T(8,128)(2,1)}, bf16[2,128,512]{1,2,0:T(8,128)(2,1)}, u32[]{:S(2)}, u32[]{:S(2)}) collective-permute-start(bf16[2,128,512]{1,2,0:T(8,128)(2,1)} %select_convert_fusion.3), channel_id=1, source_target_pairs={{0,32},{32,0},{4,36},{36,4},{8,40},{40,8},{12,44},{44,12},{16,48},... | collective-permute-start | bytes 786440 | tf_op jit(solution)/shard_map/ppermute | solution.py:21
  335.8 6.8 %collective-permute-start.9 = (bf16[2,64,512]{1,2,0:T(8,128)(2,1)S(1)}, bf16[2,64,512]{1,2,0:T(8,128)(2,1)S(1)}, u32[]{:S(2)}, u32[]{:S(2)}) collective-permute-start(bf16[2,64,512]{1,2,0:T(8,128)(2,1)S(1)} %select_convert_fusion.2), channel_id=1, source_target_pairs={{0,16},{16,0},{4,20},{20,4},{8,24},{24,8},{12,28},{28,12},{32,48},... | collective-permute-start | bytes 393224 | tf_op jit(solution)/shard_map/ppermute | solution.py:21
  338.8 4.6 collective-permute-start.7
  342.9 5.3 collective-permute-start.10
  343.6 10.9 %copy-start.80 = (pred[4,512]{1,0:T(4,128)(4,1)S(1)}, pred[4,512]{1,0:T(4,128)(4,1)}, u32[]{:S(2)}) copy-start(pred[4,512]{1,0:T(4,128)(4,1)} %copy-done.79) | copy-start | bytes 6148
  345.2 9.3 %copy-start.52 = (f32[64,512]{1,0:T(8,128)S(1)}, f32[64,512]{1,0:T(8,128)}, u32[]{:S(2)}) copy-start(f32[64,512]{1,0:T(8,128)} %copy.513) | copy-start | bytes 393220
  345.2 9.3 %copy-start.53 = (f32[64,512]{1,0:T(8,128)S(1)}, f32[64,512]{1,0:T(8,128)}, u32[]{:S(2)}) copy-start(f32[64,512]{1,0:T(8,128)} %copy.531) | copy-start | bytes 393220
  349.3 8.6 %collective-permute-start.11 = (bf16[2,16,512]{1,2,0:T(8,128)(2,1)}, bf16[2,16,512]{1,2,0:T(8,128)(2,1)}, u32[]{:S(2)}, u32[]{:S(2)}) collective-permute-start(bf16[2,16,512]{1,2,0:T(8,128)(2,1)} %select_convert_fusion), channel_id=1, source_target_pairs={{0,4},{4,0},{8,12},{12,8},{16,20},{20,16},{24,28},{28,24},{32,36},... | collective-permute-start | bytes 98312 | tf_op jit(solution)/shard_map/ppermute | solution.py:21
  (59 other events, 196.7 us)
Sparse Core Ops, SparseCore 0:
  333.3 263.0 all-reduce.1
where the time goes:
time: 614 us; the launch traced here: 605 us
  waiting for transfers between devices  237 us (39%)
  local copies, waits for them, and re-layouts  182 us (30%)
  matrix products  87 us (14%)
  other arithmetic  64.8 us (11%)
  starting transfers between devices  18.3 us (3%)
  between operations  15.3 us (2%)
    psum x1, waiting for transfers between devices, local(): weight_summed = lax.psum(weight_local, ('seq', 'dp'))  231 us
    slice x41, local copies, waits for them, and re-layouts, head_pair(): columns = array[:, :, first_head * E:(first_head + 2) * E]  37.6 us
    another operation x16, local copies, waits for them, and re-layouts  21 us
    ppermute x12, starting transfers between devices, partner(): return lax.ppermute(block, axis, route)  18.2 us
    dot_general x12, matrix products, backward_block(): jnp.einsum('shqk,sqhe->skhe', probs_low, grad_pair, preferred_element_typ...  16.9 us
    dot_general x12, matrix products, backward_block(): jnp.einsum('shqk,skhe->sqhe', scores_low, key_pair, preferred_element_typ...  16.2 us
    select_n x10, local copies, waits for them, and re-layouts, place_stats(): jnp.where(head_mask[None], array[:, None, :], jnp.asarray(filler, array.d...  15.5 us
    dot_general x12, matrix products, backward_block(): jnp.einsum('shqk,sqhe->skhe', scores_low, query_pair, preferred_element_t...  15.1 us
  transfers between devices with their start and end apart: 13, of which 5 were waited for; matrix products, arithmetic and copies ran while one was open for 26% of the time, Pallas kernels for 0%

commit v1 on v0

v1 whole, which is shorter than its diff:
```python
import jax
import jax.numpy as jnp
from jax import lax
from jax.experimental import pallas as pl
from jax.experimental.pallas import tpu as pltpu
from jax.sharding import PartitionSpec as P

XS, ZS, YS = 4, 8, 4
T = 256
E = 64
C2 = 0.125 * 1.4426950408889634
F32, BF16 = jnp.float32, jnp.bfloat16
NEG = -3.0e38


def dot(a, b):
    return lax.dot_general(a, b, (((1,), (0,)), ((), ())), preferred_element_type=F32)


def dot_nt(a, b):
    return lax.dot_general(a, b, (((1,), (1,)), ((), ())), preferred_element_type=F32)


def dot_tn(a, b):
    return lax.dot_general(a, b, (((0,), (0,)), ((), ())), preferred_element_type=F32)


def kernel(
    qkv_ref, dout_ref, w_ref, off_ref, out_ref, wg_ref,
    qkv_in, dout2, wv, perm, x, oth, sibs, sibr, kn, ns, kf, fs, qn, qf, g,
    o1, t1, m1, o2, t2, m2, o3, t3, m3, p1, pn, pf, attn,
    g1, d1, g2, d2, g3, d3, acc, nsend, nrecv, fsend, frecv,
    wgs, wgr, zsb, zr, ysb, yr,
    load_sem, sib_s, sib_r, near_s, near_r, far_s, far_r, x_s, x_r, z_s, z_r, y_s, y_r,
):
    pos = lax.axis_index("seq")
    y = lax.axis_index("dp")
    c = pos % 2
    xx = (pos // 2) % XS
    z = pos // (2 * XS)
    chip = (z % 2) * XS + xx

    def at(z_, x_, c_):
        return (z_ * XS + x_) * 2 + c_

    def far_pos(d, r):
        ch = (chip + d + 8) % 8
        return at(z - z % 2 + ch // XS, ch % XS, (c + r) % 2)

    xp = xx + 1 - 2 * (xx % 2)
    sib = at(z, xx, 1 - c)

    def near_pos(r):
        return at(z, xp, (c + r) % 2)

    y_target = at(4 * c + z // 2, xx, (z + 1) % 2)
    y_source = at(2 * (z % 4) + (c + 1) % 2, xx, z // 4)

    def remote(src, dst, send, recv, target, row=None):
        where = {"seq": target} if row is None else {"seq": target, "dp": row}
        return pltpu.make_async_remote_copy(
            src_ref=src, dst_ref=dst, send_sem=send, recv_sem=recv,
            device_id=where, device_id_type=pl.DeviceIdType.MESH,
        )

    mine = pl.multiple_of(c * 256, 256)
    theirs = pl.multiple_of((1 - c) * 256, 256)
    load_qkv = pltpu.make_async_copy(qkv_ref, qkv_in, load_sem.at[0])
    load_dout = pltpu.make_async_copy(dout_ref, dout2.at[0], load_sem.at[1])
    load_w = pltpu.make_async_copy(w_ref.at[pl.ds(mine, 256), :], wv, load_sem.at[2])
    load_qkv.start()
    load_dout.start()
    load_w.start()

    barrier = pltpu.get_barrier_semaphore()

    def greet(target, row=None):
        where = {"seq": target} if row is None else {"seq": target, "dp": row}
        pl.semaphore_signal(
            barrier, inc=1, device_id=where, device_id_type=pl.DeviceIdType.MESH
        )

    greet(sib)
    for d in range(1, 8):
        for r in range(2):
            greet(far_pos(d, r))
    for d in range(1, ZS):
        greet(at((z + d) % ZS, xx, c))
    for d in range(YS):
        greet(y_source, (y + d) % YS)

    lane = lax.broadcasted_iota(jnp.int32, (1, 128), 1)
    low_lane = lane < E
    head_mask = [low_lane.astype(F32).astype(BF16), (lane >= E).astype(F32).astype(BF16)]

    def offsets(row, half, pair):
        first = 4 * half + 2 * pair
        return jnp.where(low_lane, off_ref[row, first], off_ref[row, first + 1])

    def near_rows(array, off):
        shaped = array.reshape(4, 4, 16, 128)
        parts = [shaped[:, k] * (off == k).astype(F32).astype(array.dtype) for k in range(4)]
        return ((parts[0] + parts[1]) + (parts[2] + parts[3])).reshape(64, 128)

    def far_rows(array, off):
        shaped = array.reshape(16, 16, 128)
        total = shaped[0] * (off == 0).astype(F32).astype(array.dtype)
        for k in range(1, 16):
            total = total + shaped[k] * (off == k).astype(F32).astype(array.dtype)
        return total

    def near_spread(array, off):
        shaped = array.reshape(4, 1, 16, 128)
        parts = [jnp.where((off == k).reshape(1, 1, 1, 128), shaped, 0.0) for k in range(4)]
        return jnp.concatenate(parts, axis=1).reshape(T, 128)

    def far_spread(array, off):
        parts = [jnp.where(off == k, array, 0.0) for k in range(16)]
        return jnp.concatenate(parts, axis=0)

    row_id = lax.broadcasted_iota(jnp.int32, (T, T), 0)
    col_id = lax.broadcasted_iota(jnp.int32, (T, T), 1)
    swapped = (row_id % 16) * 16 + row_id // 16
    perm[...] = (swapped == col_id).astype(F32).astype(BF16)

    load_qkv.wait()
    for t in range(3):
        own = dot(perm[...], qkv_in[t, :, pl.ds(mine, 256)]).astype(BF16)
        x[0, t, 0] = own[:, :128]
        x[0, t, 1] = own[:, 128:]
        other = dot(perm[...], qkv_in[t, :, pl.ds(theirs, 256)]).astype(BF16)
        oth[t, 0] = other[:, :128]
        oth[t, 1] = other[:, 128:]
    for p in range(2):
        near_own, far_own = offsets(0, c, p), offsets(1, c, p)
        near_other, far_other = offsets(0, 1 - c, p), offsets(1, 1 - c, p)
        for k in range(2):
            kn[0, k, p] = near_rows(x[0, 1 + k, p], near_own)
            kf[0, k, p] = far_rows(x[0, 1 + k, p], far_own)
            ns[k, p] = near_rows(oth[1 + k, p], near_other)
            fs[k, p] = far_rows(oth[1 + k, p], far_other)
        qn[p, 0] = near_rows(x[0, 0, p], near_own)
        qf[p, 0] = far_rows(x[0, 0, p], far_own)
    pl.semaphore_wait(barrier, 15 + (ZS - 1) + YS)

    sib_copy = remote(oth, x.at[1], sib_s.at[0], sib_r.at[0], sib)
    sib_copy.start()
    near_copies = []
    for r in range(2):
        copy = remote(
            kn.at[0] if r == 0 else ns, kn.at[2 + r], near_s.at[0, r], near_r.at[0, r], near_pos(r)
        )
        copy.start()
        near_copies.append(copy)
    far_copies = []
    for d in range(1, 8):
        for r in range(2):
            slot = 2 * (d - 1) + r
            copy = remote(
                kf.at[0] if r == 0 else fs, kf.at[2 + slot],
                far_s.at[0, slot], far_r.at[0, slot], far_pos(d, r),
            )
            copy.start()
            far_copies.append(copy)
    load_dout.wait()
    dout_copy = remote(dout2.at[0], dout2.at[1], sib_s.at[1], sib_r.at[1], sib)
    dout_copy.start()

    def forward(query, key, value, probs_ref):
        probs, maxima = [], []
        for h in range(2):
            scores = dot_nt(query, key * head_mask[h])
            row_max = jnp.max(scores, axis=1, keepdims=True)
            prob = jnp.exp2((scores - row_max) * C2).astype(BF16)
            probs_ref[h] = prob
            probs.append(prob)
            maxima.append(row_max * C2)
        ones = jnp.ones((T, 128), BF16)
        right = jnp.concatenate(
            [
                jnp.concatenate([value * head_mask[h], ones * head_mask[h]], axis=1)
                for h in range(2)
            ],
            axis=0,
        )
        both = dot(jnp.concatenate(probs, axis=1), right)
        return both[:, :128], both[:, 128:], jnp.where(low_lane, maxima[0], maxima[1])

    def dense_forward(s):
        def body(p, carry):
            out, total, peak = forward(x[s, 0, p], x[s, 1, p], x[s, 2, p], p1.at[s, p])
            o1[s, p], t1[s, p], m1[s, p] = out, total, peak
            return carry

        lax.fori_loop(0, 2, body, 0)

    def grad_in(s):
        grads = dot_nt(dout2[s], wv[...]).astype(BF16)
        moved = dot(perm[...], grads).astype(BF16)
        g[s, 0] = moved[:, :128]
        g[s, 1] = moved[:, 128:]

    dense_forward(0)
    load_w.wait()
    grad_in(0)
    sib_copy.wait()
    for p in range(2):
        near_own, far_own = offsets(0, c, p), offsets(1, c, p)
        for k in range(2):
            kn[1, k, p] = near_rows(x[1, 1 + k, p], near_own)
            kf[1, k, p] = far_rows(x[1, 1 + k, p], far_own)
        qn[p, 1] = near_rows(x[1, 0, p], near_own)
        qf[p, 1] = far_rows(x[1, 0, p], far_own)
    dense_forward(1)
    dout_copy.wait()
    grad_in(1)

    for copy in near_copies:
        copy.wait()

    def near_forward(p, carry):
        out, total, peak = forward(
            qn[p].reshape(128, 128), kn[:, 0, p].reshape(T, 128), kn[:, 1, p].reshape(T, 128),
            pn.at[p],
        )
        o2[p], t2[p], m2[p] = (a.reshape(2, 64, 128) for a in (out, total, peak))
        return carry

    lax.fori_loop(0, 2, near_forward, 0)
    for copy in far_copies:
        copy.wait()

    def far_forward(p, carry):
        out, total, peak = forward(
            qf[p].reshape(32, 128), kf[:, 0, p].reshape(T, 128), kf[:, 1, p].reshape(T, 128),
            pf.at[p],
        )
        o3[p], t3[p], m3[p] = (a.reshape(2, 16, 128) for a in (out, total, peak))
        return carry

    lax.fori_loop(0, 2, far_forward, 0)

    same_head = (
        (lax.broadcasted_iota(jnp.int32, (256, 128), 0) % 128 < E)
        == (lax.broadcasted_iota(jnp.int32, (256, 128), 1) < E)
    ).astype(F32).astype(BF16)

    def combine(p, s):
        near_off, far_off = offsets(0, c, p), offsets(1, c, p)

        def near_wide(array):
            return jnp.broadcast_to(array.reshape(4, 1, 16, 128), (4, 4, 16, 128)).reshape(T, 128)

        def far_wide(array):
            return jnp.broadcast_to(array.reshape(1, 16, 128), (16, 16, 128)).reshape(T, 128)

        parts = [
            jnp.where((near_off == k).reshape(1, 1, 1, 128), m2[p, s].reshape(4, 1, 16, 128), NEG)
            for k in range(4)
        ]
        max2 = jnp.concatenate(parts, axis=1).reshape(T, 128)
        max3 = jnp.concatenate([jnp.where(far_off == k, m3[p, s], NEG) for k in range(16)], axis=0)
        max1 = m1[s, p]
        peak = jnp.maximum(jnp.maximum(max1, max2), max3)
        e1, e2, e3 = jnp.exp2(max1 - peak), jnp.exp2(max2 - peak), jnp.exp2(max3 - peak)
        denom = e1 * t1[s, p] + e2 * near_wide(t2[p, s]) + e3 * far_wide(t3[p, s])
        inverse = 1.0 / denom
        f1, f2, f3 = e1 * inverse, e2 * inverse, e3 * inverse
        mixed = f1 * o1[s, p] + f2 * near_wide(o2[p, s]) + f3 * far_wide(o3[p, s])
        low = mixed.astype(BF16)
        grads = g[s, p].astype(F32)
        product = grads * low.astype(F32)
        high = product.astype(BF16)
        rest = (product - high.astype(F32)).astype(BF16)
        dstat = dot(jnp.concatenate([high, rest], axis=1), same_head)
        g1[s, p] = (grads * f1).astype(BF16)
        d1[s, p] = dstat * f1
        g2[p, s] = near_rows(grads * f2, near_off).astype(BF16)
        d2[p, s] = near_rows(dstat * f2, near_off)
        g3[p, s] = far_rows(grads * f3, far_off).astype(BF16)
        d3[p, s] = far_rows(dstat * f3, far_off)
        return low

    for s in range(2):
        rows = jnp.concatenate([combine(p, s) for p in range(2)], axis=1)
        attn[s * T : (s + 1) * T, :] = dot(perm[...], rows).astype(BF16)

    for k in range(4):
        columns = slice(256 * k, 256 * k + 256)
        both = dot_tn(attn[0:T, :], dout2[0, :, columns])
        both = both + dot_tn(attn[T:, :], dout2[1, :, columns])
        shaped = both.astype(BF16).reshape(4, 4, 16, 256)
        for to in range(XS):
            wgs[to, :, :, columns] = shaped[:, to]
    x_copies = []
    for d in range(1, XS):
        to = (xx + d) % XS
        copy = remote(wgs.at[to], wgr.at[d - 1], x_s.at[d - 1], x_r.at[d - 1], at(z, to, c))
        copy.start()
        x_copies.append(copy)

    def backward(query, key, value, grads, dstat, probs_ref):
        scores = []
        for h in range(2):
            grad_probs = dot_nt(grads, value * head_mask[h])
            column = dstat[:, h * E : h * E + 1]
            scores.append((probs_ref[h].astype(F32) * (grad_probs - column)).astype(BF16))
        keys = jnp.concatenate([key * head_mask[h] for h in range(2)], axis=0)
        grad_q = dot(jnp.concatenate(scores, axis=1), keys) * 0.125
        queries = jnp.concatenate([query * head_mask[h] for h in range(2)], axis=0)
        grad_k = dot_tn(jnp.concatenate(scores, axis=0), queries) * 0.125
        outs = jnp.concatenate([grads * head_mask[h] for h in range(2)], axis=0)
        grad_v = dot_tn(jnp.concatenate([probs_ref[0], probs_ref[1]], axis=0), outs)
        return grad_q, grad_k, grad_v

    acc[...] = jnp.zeros_like(acc)

    def near_backward(p, carry):
        off = offsets(0, c, p)
        grad_q, grad_k, grad_v = backward(
            qn[p].reshape(128, 128), kn[:, 0, p].reshape(T, 128), kn[:, 1, p].reshape(T, 128),
            g2[p].reshape(128, 128), d2[p].reshape(128, 128), pn.at[p],
        )
        grad_q = grad_q.reshape(2, 64, 128)
        for s in range(2):
            acc[s, 0, p] = near_spread(grad_q[s], off)
        for k, part in enumerate((grad_k, grad_v)):
            part = part.reshape(4, 64, 128)
            for s in range(2):
                acc[s, 1 + k, p] = near_spread(part[s], off)
            for r in range(2):
                nsend[r, k, p] = part[2 + r].astype(BF16)
        return carry

    lax.fori_loop(0, 2, near_backward, 0)
    near_back = []
    for r in range(2):
        copy = remote(nsend.at[r], nrecv.at[r], near_s.at[1, r], near_r.at[1, r], near_pos(r))
        copy.start()
        near_back.append(copy)

    def far_backward(p, carry):
        off = offsets(1, c, p)
        grad_q, grad_k, grad_v = backward(
            qf[p].reshape(32, 128), kf[:, 0, p].reshape(T, 128), kf[:, 1, p].reshape(T, 128),
            g3[p].reshape(32, 128), d3[p].reshape(32, 128), pf.at[p],
        )
        grad_q = grad_q.reshape(2, 16, 128)
        for s in range(2):
            acc[s, 0, p] += far_spread(grad_q[s], off)
        for k, part in enumerate((grad_k, grad_v)):
            part = part.reshape(16, 16, 128)
            for s in range(2):
                acc[s, 1 + k, p] += far_spread(part[s], off)
            fsend[:, k, p] = part[2:].astype(BF16)
        return carry

    lax.fori_loop(0, 2, far_backward, 0)
    far_back = []
    for d in range(1, 8):
        for r in range(2):
            slot = 2 * (d - 1) + r
            copy = remote(
                fsend.at[slot], frecv.at[slot],
                far_s.at[1, slot], far_r.at[1, slot], far_pos(-d, r),
            )
            copy.start()
            far_back.append(copy)

    def dense_backward(s):
        def body(p, carry):
            grad_parts = backward(
                x[s, 0, p], x[s, 1, p], x[s, 2, p], g1[s, p], d1[s, p], p1.at[s, p]
            )
            for t, part in enumerate(grad_parts):
                if s == 1:
                    sibs[t, p] = (acc[s, t, p] + part).astype(BF16)
                else:
                    acc[s, t, p] += part
            return carry

        lax.fori_loop(0, 2, body, 0)

    dense_backward(1)
    sib_back = remote(sibs, sibr, sib_s.at[2], sib_r.at[2], sib)
    sib_back.start()

    for copy in x_copies:
        copy.wait()
    total = wgs[xx].astype(F32)
    for d in range(XS - 1):
        total = total + wgr[d].astype(F32)
    for k in range(ZS):
        chunk = total[k // 2, 8 * ((k + 1) % 2) : 8 * ((k + 1) % 2) + 8]
        zsb[k] = jnp.concatenate([chunk[:, :512], chunk[:, 512:]], axis=0).astype(BF16)
    z_copies = []
    for d in range(1, ZS):
        to = (z + d) % ZS
        copy = remote(zsb.at[to], zr.at[d - 1], z_s.at[d - 1], z_r.at[d - 1], at(to, xx, c))
        copy.start()
        z_copies.append(copy)

    dense_backward(0)

    for copy in z_copies:
        copy.wait()
    total = zsb[z].astype(F32)
    for d in range(ZS - 1):
        total = total + zr[d].astype(F32)
    ysb[...] = total
    y_copies = []
    for d in range(YS):
        copy = remote(ysb, yr.at[d], y_s.at[d], y_r.at[d], y_target, (y + d) % YS)
        copy.start()
        y_copies.append(copy)

    for copy in near_back:
        copy.wait()
    for copy in far_back:
        copy.wait()

    def returned(t, p, r):
        half = c if r == 0 else 1 - c
        near = near_spread(nrecv[r, t - 1, p].astype(F32), offsets(0, half, p))
        far = frecv[r, t - 1, p].astype(F32)
        for d in range(1, 7):
            far = far + frecv[2 * d + r, t - 1, p].astype(F32)
        return near + far_spread(far, offsets(1, half, p))

    def write(t, columns, parts):
        joined = jnp.concatenate([part.astype(BF16) for part in parts], axis=1)
        out_ref[t, :, pl.ds(columns, 256)] = dot(perm[...], joined).astype(BF16)

    for t in range(3):
        parts = [acc[0, t, p] for p in range(2)]
        if t > 0:
            parts = [parts[p] + returned(t, p, 0) for p in range(2)]
        write(t, mine, parts)
    sib_back.wait()
    for t in range(3):
        parts = [sibr[t, p].astype(F32) for p in range(2)]
        if t > 0:
            parts = [parts[p] + returned(t, p, 1) for p in range(2)]
        write(t, theirs, parts)
    for copy in y_copies:
        copy.wait()
    total = ((yr[0] + yr[1]) + (yr[2] + yr[3])) * (1.0 / YS)
    wg_ref[:, :512] = total[:8]
    wg_ref[:, 512:] = total[8:]


def local(qkv, dout, out_weight, head_offsets):
    planes = jnp.transpose(qkv[0], (1, 0, 2))
    vmem = pltpu.VMEM
    dma = pltpu.SemaphoreType.DMA
    grads, weight_grad = pl.pallas_call(
        kernel,
        out_shape=(
            jax.ShapeDtypeStruct((3, T, 512), BF16),
            jax.ShapeDtypeStruct((8, 1024), F32),
        ),
        in_specs=[
            pl.BlockSpec(memory_space=pl.ANY),
            pl.BlockSpec(memory_space=pl.ANY),
            pl.BlockSpec(memory_space=pl.ANY),
            pl.BlockSpec(memory_space=pltpu.SMEM),
        ],
        out_specs=(pl.BlockSpec(memory_space=pltpu.VMEM), pl.BlockSpec(memory_space=pltpu.VMEM)),
        scratch_shapes=[
            vmem((3, T, 512), BF16),
            vmem((2, T, 1024), BF16),
            vmem((256, 1024), BF16),
            vmem((T, T), BF16),
            vmem((2, 3, 2, T, 128), BF16),
            vmem((3, 2, T, 128), BF16),
            vmem((3, 2, T, 128), BF16),
            vmem((3, 2, T, 128), BF16),
            vmem((4, 2, 2, 64, 128), BF16),
            vmem((2, 2, 64, 128), BF16),
            vmem((16, 2, 2, 16, 128), BF16),
            vmem((2, 2, 16, 128), BF16),
            vmem((2, 2, 64, 128), BF16),
            vmem((2, 2, 16, 128), BF16),
            vmem((2, 2, T, 128), BF16),
            *[vmem((2, 2, T, 128), F32)] * 3,
            *[vmem((2, 2, 64, 128), F32)] * 3,
            *[vmem((2, 2, 16, 128), F32)] * 3,
            vmem((2, 2, 2, T, T), BF16),
            vmem((2, 2, 128, T), BF16),
            vmem((2, 2, 32, T), BF16),
            vmem((2 * T, 256), BF16),
            vmem((2, 2, T, 128), BF16),
            vmem((2, 2, T, 128), F32),
            vmem((2, 2, 64, 128), BF16),
            vmem((2, 2, 64, 128), F32),
            vmem((2, 2, 16, 128), BF16),
            vmem((2, 2, 16, 128), F32),
            vmem((2, 3, 2, T, 128), F32),
            vmem((2, 2, 2, 64, 128), BF16),
            vmem((2, 2, 2, 64, 128), BF16),
            vmem((14, 2, 2, 16, 128), BF16),
            vmem((14, 2, 2, 16, 128), BF16),
            vmem((4, 4, 16, 1024), BF16),
            vmem((3, 4, 16, 1024), BF16),
            vmem((8, 16, 512), BF16),
            vmem((7, 16, 512), BF16),
            vmem((16, 512), F32),
            vmem((4, 16, 512), F32),
            dma((3,)),
            dma((3,)), dma((3,)),
            dma((2, 2)), dma((2, 2)),
            dma((2, 14)), dma((2, 14)),
            dma((3,)), dma((3,)),
            dma((7,)), dma((7,)),
            dma((4,)), dma((4,)),
        ],
        compiler_params=pltpu.CompilerParams(
            collective_id=0, has_side_effects=True, vmem_limit_bytes=48 * 1024 * 1024
        ),
        cost_estimate=pl.CostEstimate(
            flops=1_200_000_000, bytes_accessed=4_000_000, transcendentals=700_000
        ),
    )(planes, dout[0], out_weight, head_offsets)
    return jnp.transpose(grads, (1, 0, 2))[None], weight_grad


def solution(mesh):
    return jax.shard_map(
        local,
        mesh=mesh,
        in_specs=(P("dp", "seq", None, None), P("dp", "seq", None), P(), P()),
        out_specs=(P("dp", "seq", None, None), P("seq", None)),
        check_vma=False,
    )
```

time: 614 us -> 52.4 us (0.09)
  the two profiles are of different devices: /device:TPU:1 before, /device:TPU:65 now
where the time goes in v1:
time: 52.4 us; the launch traced here: 52.1 us
  Pallas kernels  45.9 us (88%)
  local copies, waits for them, and re-layouts  5.57 us (11%)
  between operations  0.65 us (1%)
    pallas_call x1, Pallas kernels, local(): pl.pallas_call(kernel, out_shape=(jax.ShapeDtypeStruct((3, T, 512), BF16)...  45.9 us
    unnamed x10, local copies, waits for them, and re-layouts  5.57 us

profile of v1, /device:TPU:65, one launch (start us, length us, event | category | flops | bytes accessed | tf_op | source)
XLA Modules:
  0.0 52.1 jit_solution(15042465648843719684)
XLA Ops:
  0.6 0.0 copy-start.3
  0.6 0.7 %copy-done.3 = s32[2,8]{1,0:T(2,128)S(1)} copy-done((s32[2,8]{1,0:T(2,128)S(1)}, s32[2,8]{1,0:T(2,128)}, u32[]{:S(2)}) %copy-start.3) | copy-done | bytes 88
  1.3 0.0 copy-start
  1.3 1.2 %copy-done = bf16[512,1024]{1,0:T(8,128)(2,1)S(1)} copy-done((bf16[512,1024]{1,0:T(8,128)(2,1)S(1)}, bf16[512,1024]{1,0:T(8,128)(2,1)}, u32[]{:S(2)}) %copy-start) | copy-done | bytes 1048600
  2.5 0.0 copy-start.1
  2.5 1.1 %copy-done.1 = bf16[1,256,3,512]{3,1,2,0:T(8,128)(2,1)S(1)} copy-done((bf16[1,256,3,512]{3,1,2,0:T(8,128)(2,1)S(1)}, bf16[1,256,3,512]{3,1,2,0:T(8,128)(2,1)}, u32[]{:S(2)}) %copy-start.1) | copy-done | bytes 786456
  3.7 0.0 copy-start.2
  3.7 1.0 %copy-done.2 = bf16[1,256,1024]{2,1,0:T(8,128)(2,1)S(1)} copy-done((bf16[1,256,1024]{2,1,0:T(8,128)(2,1)S(1)}, bf16[1,256,1024]{2,1,0:T(8,128)(2,1)}, u32[]{:S(2)}) %copy-start.2) | copy-done | bytes 524312
  4.7 45.9 %shard_map.59 = (bf16[3,256,512]{2,1,0:T(8,128)(2,1)S(1)}, f32[8,1024]{1,0:T(8,128)S(1)}) custom-call(bf16[3,256,512]{2,1,0:T(8,128)(2,1)S(1)} %bitcast.8, bf16[256,1024]{1,0:T(8,128)(2,1)S(1)} %bitcast.9, bf16[512,1024]{1,0:T(8,128)(2,1)S(1)} %copy-done, s32[2,8]{1,0:T(2,128)S(1)} %copy-done.3), custom_call_target="tpu_custom_call" | custom-call | flops 1200000000 | bytes 4000000 | tf_op jit(solution)/shard_map/pallas_call | solution.py:456
  50.6 0.9 %copy.8 = bf16[1,256,3,512]{3,1,2,0:T(8,128)(2,1)} copy(bf16[1,256,3,512]{3,1,2,0:T(8,128)(2,1)S(1)} %bitcast.7) | data formatting | bytes 1572864
  51.5 0.6 %copy.9 = f32[8,1024]{1,0:T(8,128)} copy(f32[8,1024]{1,0:T(8,128)S(1)} %get-tuple-element.9) | data formatting | bytes 65536
Async XLA Ops:
  0.6 0.7 %copy-start.3 = (s32[2,8]{1,0:T(2,128)S(1)}, s32[2,8]{1,0:T(2,128)}, u32[]{:S(2)}) copy-start(s32[2,8]{1,0:T(2,128)} %off_ref.1) | copy-start | bytes 196
  1.3 1.2 %copy-start = (bf16[512,1024]{1,0:T(8,128)(2,1)S(1)}, bf16[512,1024]{1,0:T(8,128)(2,1)}, u32[]{:S(2)}) copy-start(bf16[512,1024]{1,0:T(8,128)(2,1)} %w_ref.1) | copy-start | bytes 3145732
  2.5 1.1 %copy-start.1 = (bf16[1,256,3,512]{3,1,2,0:T(8,128)(2,1)S(1)}, bf16[1,256,3,512]{3,1,2,0:T(8,128)(2,1)}, u32[]{:S(2)}) copy-start(bf16[1,256,3,512]{3,1,2,0:T(8,128)(2,1)} %param.4) | copy-start | bytes 2359300
  3.7 1.0 %copy-start.2 = (bf16[1,256,1024]{2,1,0:T(8,128)(2,1)S(1)}, bf16[1,256,1024]{2,1,0:T(8,128)(2,1)}, u32[]{:S(2)}) copy-start(bf16[1,256,1024]{2,1,0:T(8,128)(2,1)} %param.5) | copy-start | bytes 1572868

commit v2 on v1

--- a/solution.py
+++ b/solution.py
@@ -26,12 +26,12 @@
 
 
 def kernel(
-    qkv_ref, dout_ref, w_ref, off_ref, out_ref, wg_ref,
+    qkv_ref, dout_ref, w_ref, off_hbm, out_ref, wg_ref,
     qkv_in, dout2, wv, perm, x, oth, sibs, sibr, kn, ns, kf, fs, qn, qf, g,
     o1, t1, m1, o2, t2, m2, o3, t3, m3, p1, pn, pf, attn,
-    g1, d1, g2, d2, g3, d3, acc, nsend, nrecv, fsend, frecv,
-    wgs, wgr, zsb, zr, ysb, yr,
-    load_sem, sib_s, sib_r, near_s, near_r, far_s, far_r, x_s, x_r, z_s, z_r, y_s, y_r,
+    g1, q1, f1s, d1, gn, g2, q2, f2s, d2, gf, g3, q3, f3s, d3,
+    acc, nsend, nrecv, fsend, frecv, wgs, wgr, zsb, zr, off_ref,
+    load_sem, sib_s, sib_r, near_s, near_r, far_s, far_r, xy_s, xy_r, zy_s, zy_r, known,
 ):
     pos = lax.axis_index("seq")
     y = lax.axis_index("dp")
@@ -53,8 +53,10 @@
     def near_pos(r):
         return at(z, xp, (c + r) % 2)
 
-    y_target = at(4 * c + z // 2, xx, (z + 1) % 2)
-    y_source = at(2 * (z % 4) + (c + 1) % 2, xx, z // 4)
+    z_outer = (z + 2 * (z % 2) - 1 + ZS) % ZS
+
+    def z_pos(d):
+        return at((z + d + ZS) % ZS, xx, c)
 
     def remote(src, dst, send, recv, target, row=None):
         where = {"seq": target} if row is None else {"seq": target, "dp": row}
@@ -68,26 +70,27 @@
     load_qkv = pltpu.make_async_copy(qkv_ref, qkv_in, load_sem.at[0])
     load_dout = pltpu.make_async_copy(dout_ref, dout2.at[0], load_sem.at[1])
     load_w = pltpu.make_async_copy(w_ref.at[pl.ds(mine, 256), :], wv, load_sem.at[2])
+    load_off = pltpu.make_async_copy(off_hbm, off_ref, load_sem.at[3])
     load_qkv.start()
+    load_off.start()
     load_dout.start()
     load_w.start()
 
     barrier = pltpu.get_barrier_semaphore()
 
-    def greet(target, row=None):
+    def tell(semaphore, target, row=None):
         where = {"seq": target} if row is None else {"seq": target, "dp": row}
         pl.semaphore_signal(
-            barrier, inc=1, device_id=where, device_id_type=pl.DeviceIdType.MESH
-        )
-
-    greet(sib)
-    for d in range(1, 8):
+            semaphore, inc=1, device_id=where, device_id_type=pl.DeviceIdType.MESH
+        )
+
+    tell(barrier, at(z_outer, xx, c))
+    for d in range(1, YS):
+        tell(barrier, pos, (y + d) % YS)
+    for d in range(7, 0, -1):
         for r in range(2):
-            greet(far_pos(d, r))
-    for d in range(1, ZS):
-        greet(at((z + d) % ZS, xx, c))
-    for d in range(YS):
-        greet(y_source, (y + d) % YS)
+            tell(barrier, far_pos(d, r))
+    tell(barrier, sib)
 
     lane = lax.broadcasted_iota(jnp.int32, (1, 128), 1)
     low_lane = lane < E
@@ -123,6 +126,7 @@
     swapped = (row_id % 16) * 16 + row_id // 16
     perm[...] = (swapped == col_id).astype(F32).astype(BF16)
 
+    load_off.wait()
     load_qkv.wait()
     for t in range(3):
         own = dot(perm[...], qkv_in[t, :, pl.ds(mine, 256)]).astype(BF16)
@@ -141,7 +145,7 @@
             fs[k, p] = far_rows(oth[1 + k, p], far_other)
         qn[p, 0] = near_rows(x[0, 0, p], near_own)
         qf[p, 0] = far_rows(x[0, 0, p], far_own)
-    pl.semaphore_wait(barrier, 15 + (ZS - 1) + YS)
+    pl.semaphore_wait(barrier, 15 + (YS - 1) + 1)
 
     sib_copy = remote(oth, x.at[1], sib_s.at[0], sib_r.at[0], sib)
     sib_copy.start()
@@ -165,6 +169,8 @@
     load_dout.wait()
     dout_copy = remote(dout2.at[0], dout2.at[1], sib_s.at[1], sib_r.at[1], sib)
     dout_copy.start()
+    for d in (-1, 1):
+        tell(known.at[0], z_pos(d))
 
     def forward(query, key, value, probs_ref):
         probs, maxima = [], []
@@ -212,6 +218,9 @@
         qn[p, 1] = near_rows(x[1, 0, p], near_own)
         qf[p, 1] = far_rows(x[1, 0, p], far_own)
     dense_forward(1)
+    pl.semaphore_wait(known.at[0], 2)
+    for d in (-2, 2):
+        tell(known.at[1], z_pos(d))
     dout_copy.wait()
     grad_in(1)
 
@@ -229,6 +238,8 @@
     lax.fori_loop(0, 2, near_forward, 0)
     for copy in far_copies:
         copy.wait()
+    pl.semaphore_wait(known.at[1], 2)
+    tell(known.at[2], sib)
 
     def far_forward(p, carry):
         out, total, peak = forward(
@@ -269,57 +280,72 @@
         mixed = f1 * o1[s, p] + f2 * near_wide(o2[p, s]) + f3 * far_wide(o3[p, s])
         low = mixed.astype(BF16)
         grads = g[s, p].astype(F32)
+        query = x[s, 0, p].astype(F32)
         product = grads * low.astype(F32)
         high = product.astype(BF16)
         rest = (product - high.astype(F32)).astype(BF16)
         dstat = dot(jnp.concatenate([high, rest], axis=1), same_head)
         g1[s, p] = (grads * f1).astype(BF16)
-        d1[s, p] = dstat * f1
-        g2[p, s] = near_rows(grads * f2, near_off).astype(BF16)
-        d2[p, s] = near_rows(dstat * f2, near_off)
-        g3[p, s] = far_rows(grads * f3, far_off).astype(BF16)
-        d3[p, s] = far_rows(dstat * f3, far_off)
+        q1[s, p] = (query * f1).astype(BF16)
+        f1s[s, p] = f1
+        d1[s, p] = dstat
+        near_f, near_g = near_rows(f2, near_off), near_rows(g[s, p], near_off)
+        gn[p, s] = near_g
+        g2[p, s] = (near_g.astype(F32) * near_f).astype(BF16)
+        q2[p, s] = (qn[p, s].astype(F32) * near_f).astype(BF16)
+        f2s[p, s] = near_f
+        d2[p, s] = near_rows(dstat, near_off)
+        far_f, far_g = far_rows(f3, far_off), far_rows(g[s, p], far_off)
+        gf[p, s] = far_g
+        g3[p, s] = (far_g.astype(F32) * far_f).astype(BF16)
+        q3[p, s] = (qf[p, s].astype(F32) * far_f).astype(BF16)
+        f3s[p, s] = far_f
+        d3[p, s] = far_rows(dstat, far_off)
         return low
 
     for s in range(2):
         rows = jnp.concatenate([combine(p, s) for p in range(2)], axis=1)
         attn[s * T : (s + 1) * T, :] = dot(perm[...], rows).astype(BF16)
 
-    for k in range(4):
+    pl.semaphore_wait(known.at[2], 1)
+    for k in range(YS):
         columns = slice(256 * k, 256 * k + 256)
         both = dot_tn(attn[0:T, :], dout2[0, :, columns])
         both = both + dot_tn(attn[T:, :], dout2[1, :, columns])
-        shaped = both.astype(BF16).reshape(4, 4, 16, 256)
+        shaped = both.astype(BF16).reshape(4, XS, 16, 256)
         for to in range(XS):
-            wgs[to, :, :, columns] = shaped[:, to]
-    x_copies = []
-    for d in range(1, XS):
-        to = (xx + d) % XS
-        copy = remote(wgs.at[to], wgr.at[d - 1], x_s.at[d - 1], x_r.at[d - 1], at(z, to, c))
-        copy.start()
-        x_copies.append(copy)
-
-    def backward(query, key, value, grads, dstat, probs_ref):
+            wgs[to, k] = shaped[:, to]
+    xy_copies = []
+    for dx in range(XS):
+        for dy in range(YS):
+            if dx + dy > 0:
+                slot = dx * YS + dy - 1
+                tx, ty = (xx + dx) % XS, (y + dy) % YS
+                copy = remote(
+                    wgs.at[tx, ty], wgr.at[slot], xy_s.at[slot], xy_r.at[slot], at(z, tx, c), ty
+                )
+                copy.start()
+                xy_copies.append(copy)
+
+    def backward(key, value, grads, dstat, factor, query_f, grads_f, probs_ref):
         scores = []
         for h in range(2):
             grad_probs = dot_nt(grads, value * head_mask[h])
             column = dstat[:, h * E : h * E + 1]
             scores.append((probs_ref[h].astype(F32) * (grad_probs - column)).astype(BF16))
         keys = jnp.concatenate([key * head_mask[h] for h in range(2)], axis=0)
-        grad_q = dot(jnp.concatenate(scores, axis=1), keys) * 0.125
-        queries = jnp.concatenate([query * head_mask[h] for h in range(2)], axis=0)
+        grad_q = dot(jnp.concatenate(scores, axis=1), keys) * (factor * 0.125)
+        queries = jnp.concatenate([query_f * head_mask[h] for h in range(2)], axis=0)
         grad_k = dot_tn(jnp.concatenate(scores, axis=0), queries) * 0.125
-        outs = jnp.concatenate([grads * head_mask[h] for h in range(2)], axis=0)
+        outs = jnp.concatenate([grads_f * head_mask[h] for h in range(2)], axis=0)
         grad_v = dot_tn(jnp.concatenate([probs_ref[0], probs_ref[1]], axis=0), outs)
         return grad_q, grad_k, grad_v
-
-    acc[...] = jnp.zeros_like(acc)
 
     def near_backward(p, carry):
         off = offsets(0, c, p)
         grad_q, grad_k, grad_v = backward(
-            qn[p].reshape(128, 128), kn[:, 0, p].reshape(T, 128), kn[:, 1, p].reshape(T, 128),
-            g2[p].reshape(128, 128), d2[p].reshape(128, 128), pn.at[p],
+            kn[:, 0, p].reshape(T, 128), kn[:, 1, p].reshape(T, 128),
+            *(a[p].reshape(128, 128) for a in (gn, d2, f2s, q2, g2)), pn.at[p],
         )
         grad_q = grad_q.reshape(2, 64, 128)
         for s in range(2):
@@ -342,8 +368,8 @@
     def far_backward(p, carry):
         off = offsets(1, c, p)
         grad_q, grad_k, grad_v = backward(
-            qf[p].reshape(32, 128), kf[:, 0, p].reshape(T, 128), kf[:, 1, p].reshape(T, 128),
-            g3[p].reshape(32, 128), d3[p].reshape(32, 128), pf.at[p],
+            kf[:, 0, p].reshape(T, 128), kf[:, 1, p].reshape(T, 128),
+            *(a[p].reshape(32, 128) for a in (gf, d3, f3s, q3, g3)), pf.at[p],
         )
         grad_q = grad_q.reshape(2, 16, 128)
         for s in range(2):
@@ -370,7 +396,8 @@
     def dense_backward(s):
         def body(p, carry):
             grad_parts = backward(
-                x[s, 0, p], x[s, 1, p], x[s, 2, p], g1[s, p], d1[s, p], p1.at[s, p]
+                x[s, 1, p], x[s, 2, p], g[s, p], d1[s, p], f1s[s, p], q1[s, p], g1[s, p],
+                p1.at[s, p],
             )
             for t, part in enumerate(grad_parts):
                 if s == 1:
@@ -385,34 +412,39 @@
     sib_back = remote(sibs, sibr, sib_s.at[2], sib_r.at[2], sib)
     sib_back.start()
 
-    for copy in x_copies:
+    dense_backward(0)
+
+    for copy in xy_copies:
         copy.wait()
-    total = wgs[xx].astype(F32)
-    for d in range(XS - 1):
+    total = wgs[xx, y].astype(F32)
+    for d in range(XS * YS - 1):
         total = total + wgr[d].astype(F32)
-    for k in range(ZS):
-        chunk = total[k // 2, 8 * ((k + 1) % 2) : 8 * ((k + 1) % 2) + 8]
-        zsb[k] = jnp.concatenate([chunk[:, :512], chunk[:, 512:]], axis=0).astype(BF16)
-    z_copies = []
-    for d in range(1, ZS):
-        to = (z + d) % ZS
-        copy = remote(zsb.at[to], zr.at[d - 1], z_s.at[d - 1], z_r.at[d - 1], at(to, xx, c))
-        copy.start()
-        z_copies.append(copy)
-
-    dense_backward(0)
-
-    for copy in z_copies:
-        copy.wait()
-    total = zsb[z].astype(F32)
-    for d in range(ZS - 1):
-        total = total + zr[d].astype(F32)
-    ysb[...] = total
-    y_copies = []
-    for d in range(YS):
-        copy = remote(ysb, yr.at[d], y_s.at[d], y_r.at[d], y_target, (y + d) % YS)
-        copy.start()
-        y_copies.append(copy)
+    for a in range(4):
+        for half in range(2):
+            chunk = total[a, 8 * half : 8 * half + 8]
+            zsb[a, half] = jnp.concatenate([chunk[:, :128], chunk[:, 128:]], axis=0).astype(BF16)
+    zy_copies = []
+    for dy in range(YS):
+        for a in range(4):
+            for half in range(2):
+                target = at(4 * c + a, xx, half)
+                source, landing = zsb.at[a, half], zr.at[dy, z]
+                copy = remote(
+                    source, landing, zy_s.at[dy, a, half], zy_r.at[dy, z], target, (y + dy) % YS
+                )
+                if dy > 0:
+                    copy.start()
+                else:
+
+                    @pl.when(target != pos)
+                    def _(copy=copy):
+                        copy.start()
+
+                    @pl.when(target == pos)
+                    def _(source=source, landing=landing):
+                        pltpu.make_async_copy(source, landing, zy_r.at[0, z]).start()
+
+                zy_copies.append((copy, dy, target))
 
     for copy in near_back:
         copy.wait()
@@ -442,11 +474,26 @@
         if t > 0:
             parts = [parts[p] + returned(t, p, 1) for p in range(2)]
         write(t, theirs, parts)
-    for copy in y_copies:
-        copy.wait()
-    total = ((yr[0] + yr[1]) + (yr[2] + yr[3])) * (1.0 / YS)
-    wg_ref[:, :512] = total[:8]
-    wg_ref[:, 512:] = total[8:]
+    for copy, dy, target in zy_copies:
+        if dy > 0:
+            copy.wait_send()
+        else:
+
+            @pl.when(target != pos)
+            def _(copy=copy):
+                copy.wait_send()
+
+    for dy in range(YS):
+        total = jnp.zeros((16, 128), F32)
+        for k in range(ZS):
+            arrived = zr.at[dy, k]
+            remote(arrived, arrived, zy_s.at[0, 0, 0], zy_r.at[dy, k], sib).wait_recv()
+        for k in range(ZS):
+            total = total + zr[dy, k].astype(F32)
+        total = total * (1.0 / YS)
+        first = 256 * ((y - dy + YS) % YS)
+        wg_ref[:, pl.ds(pl.multiple_of(first, 128), 128)] = total[:8]
+        wg_ref[:, pl.ds(pl.multiple_of(first + 128, 128), 128)] = total[8:]
 
 
 def local(qkv, dout, out_weight, head_offsets):
@@ -460,10 +507,10 @@
             jax.ShapeDtypeStruct((8, 1024), F32),
         ),
         in_specs=[
-            pl.BlockSpec(memory_space=pl.ANY),
-            pl.BlockSpec(memory_space=pl.ANY),
-            pl.BlockSpec(memory_space=pl.ANY),
-            pl.BlockSpec(memory_space=pltpu.SMEM),
+            pl.BlockSpec(memory_space=pltpu.HBM),
+            pl.BlockSpec(memory_space=pltpu.HBM),
+            pl.BlockSpec(memory_space=pltpu.HBM),
+            pl.BlockSpec(memory_space=pltpu.HBM),
         ],
         out_specs=(pl.BlockSpec(memory_space=pltpu.VMEM), pl.BlockSpec(memory_space=pltpu.VMEM)),
         scratch_shapes=[
@@ -489,33 +536,32 @@
             vmem((2, 2, 128, T), BF16),
             vmem((2, 2, 32, T), BF16),
             vmem((2 * T, 256), BF16),
-            vmem((2, 2, T, 128), BF16),
-            vmem((2, 2, T, 128), F32),
-            vmem((2, 2, 64, 128), BF16),
-            vmem((2, 2, 64, 128), F32),
-            vmem((2, 2, 16, 128), BF16),
-            vmem((2, 2, 16, 128), F32),
+            *[vmem((2, 2, T, 128), BF16)] * 2,
+            *[vmem((2, 2, T, 128), F32)] * 2,
+            *[vmem((2, 2, 64, 128), BF16)] * 3,
+            *[vmem((2, 2, 64, 128), F32)] * 2,
+            *[vmem((2, 2, 16, 128), BF16)] * 3,
+            *[vmem((2, 2, 16, 128), F32)] * 2,
             vmem((2, 3, 2, T, 128), F32),
             vmem((2, 2, 2, 64, 128), BF16),
             vmem((2, 2, 2, 64, 128), BF16),
             vmem((14, 2, 2, 16, 128), BF16),
             vmem((14, 2, 2, 16, 128), BF16),
-            vmem((4, 4, 16, 1024), BF16),
-            vmem((3, 4, 16, 1024), BF16),
-            vmem((8, 16, 512), BF16),
-            vmem((7, 16, 512), BF16),
-            vmem((16, 512), F32),
-            vmem((4, 16, 512), F32),
-            dma((3,)),
+            vmem((4, 4, 4, 16, 256), BF16),
+            vmem((15, 4, 16, 256), BF16),
+            vmem((4, 2, 16, 128), BF16),
+            vmem((4, 8, 16, 128), BF16),
+            pltpu.SMEM((2, 8), jnp.int32),
+            dma((4,)),
             dma((3,)), dma((3,)),
             dma((2, 2)), dma((2, 2)),
             dma((2, 14)), dma((2, 14)),
-            dma((3,)), dma((3,)),
-            dma((7,)), dma((7,)),
-            dma((4,)), dma((4,)),
+            dma((15,)), dma((15,)),
+            dma((4, 4, 2)), dma((4, 8)),
+            pltpu.SemaphoreType.REGULAR((3,)),
         ],
         compiler_params=pltpu.CompilerParams(
-            collective_id=0, has_side_effects=True, vmem_limit_bytes=48 * 1024 * 1024
+            collective_id=0, has_side_effects=True, vmem_limit_bytes=60 * 1024 * 1024
         ),
         cost_estimate=pl.CostEstimate(
             flops=1_200_000_000, bytes_accessed=4_000_000, transcendentals=700_000

time: 52.4 us -> 44.7 us (0.85)
  the two profiles are of different devices: /device:TPU:65 before, /device:TPU:1 now
where the time goes in v2:
time: 44.7 us; the launch traced here: 44.6 us
  Pallas kernels  41.2 us (92%)
  local copies, waits for them, and re-layouts  2.69 us (6%)
  between operations  0.65 us (1%)
    pallas_call x1, Pallas kernels, local(): pl.pallas_call(kernel, out_shape=(jax.ShapeDtypeStruct((3, T, 512), BF16)...  41.2 us
    unnamed x4, local copies, waits for them, and re-layouts  2.69 us

profile of v2, /device:TPU:1, one launch (start us, length us, event | category | flops | bytes accessed | tf_op | source)
XLA Modules:
  0.0 44.6 jit_solution(14591149834206766300)
XLA Ops:
  0.6 41.2 %shard_map.59 = (bf16[3,256,512]{2,1,0:T(8,128)(2,1)}, f32[8,1024]{1,0:T(8,128)}) custom-call(bf16[3,256,512]{2,1,0:T(8,128)(2,1)} %bitcast.8, bf16[256,1024]{1,0:T(8,128)(2,1)} %bitcast.9, bf16[512,1024]{1,0:T(8,128)(2,1)} %w_ref.1, s32[2,8]{1,0:T(2,128)} %off_hbm.1), custom_call_target="tpu_custom_call" | custom-call | flops 1200000000 | bytes 4000000 | tf_op jit(solution)/shard_map/pallas_call | solution.py:503
  41.9 0.0 copy-start
  41.9 2.1 %copy.8 = bf16[1,256,3,512]{3,1,2,0:T(8,128)(2,1)} copy(bf16[1,256,3,512]{3,1,2,0:T(8,128)(2,1)} %bitcast.7) | data formatting | bytes 1572864
  44.0 0.0 copy-done
  44.0 0.6 %copy.9 = f32[8,1024]{1,0:T(8,128)} copy(f32[8,1024]{1,0:T(8,128)S(1)} %copy-done) | data formatting | bytes 65536
Async XLA Ops:
  41.9 2.1 %copy-start = (f32[8,1024]{1,0:T(8,128)S(1)}, f32[8,1024]{1,0:T(8,128)}, u32[]{:S(2)}) copy-start(f32[8,1024]{1,0:T(8,128)} %get-tuple-element.9) | copy-start | bytes 98308

commit v3 on v2

--- a/solution.py
+++ b/solution.py
@@ -362,7 +362,6 @@
     near_back = []
     for r in range(2):
         copy = remote(nsend.at[r], nrecv.at[r], near_s.at[1, r], near_r.at[1, r], near_pos(r))
-        copy.start()
         near_back.append(copy)
 
     def far_backward(p, carry):
@@ -390,7 +389,6 @@
                 fsend.at[slot], frecv.at[slot],
                 far_s.at[1, slot], far_r.at[1, slot], far_pos(-d, r),
             )
-            copy.start()
             far_back.append(copy)
 
     def dense_backward(s):
@@ -415,7 +413,11 @@
     dense_backward(0)
 
     for copy in xy_copies:
-        copy.wait()
+        copy.wait_send()
+    for copy in near_back + far_back:
+        copy.start()
+    for copy in xy_copies:
+        copy.wait_recv()
     total = wgs[xx, y].astype(F32)
     for d in range(XS * YS - 1):
         total = total + wgr[d].astype(F32)
@@ -496,6 +498,15 @@
         wg_ref[:, pl.ds(pl.multiple_of(first + 128, 128), 128)] = total[8:]
 
 
+def deliver(grads_ref, weight_ref, out_ref, wg_ref, sem):
+    first = pltpu.make_async_copy(grads_ref, out_ref, sem.at[0])
+    second = pltpu.make_async_copy(weight_ref, wg_ref, sem.at[1])
+    first.start()
+    second.start()
+    first.wait()
+    second.wait()
+
+
 def local(qkv, dout, out_weight, head_offsets):
     planes = jnp.transpose(qkv[0], (1, 0, 2))
     vmem = pltpu.VMEM
@@ -503,8 +514,8 @@
     grads, weight_grad = pl.pallas_call(
         kernel,
         out_shape=(
-            jax.ShapeDtypeStruct((3, T, 512), BF16),
-            jax.ShapeDtypeStruct((8, 1024), F32),
+            pltpu.VMEM((3, T, 512), BF16),
+            pltpu.VMEM((8, 1024), F32),
         ),
         in_specs=[
             pl.BlockSpec(memory_space=pltpu.HBM),
@@ -567,6 +578,17 @@
             flops=1_200_000_000, bytes_accessed=4_000_000, transcendentals=700_000
         ),
     )(planes, dout[0], out_weight, head_offsets)
+    grads, weight_grad = pl.pallas_call(
+        deliver,
+        out_shape=(
+            jax.ShapeDtypeStruct((3, T, 512), BF16),
+            jax.ShapeDtypeStruct((8, 1024), F32),
+        ),
+        in_specs=[pl.BlockSpec(memory_space=pl.ANY)] * 2,
+        out_specs=[pl.BlockSpec(memory_space=pltpu.HBM)] * 2,
+        scratch_shapes=[dma((2,))],
+        compiler_params=pltpu.CompilerParams(vmem_limit_bytes=2 * 1024 * 1024),
+    )(grads, weight_grad)
     return jnp.transpose(grads, (1, 0, 2))[None], weight_grad
 
 

time: 44.7 us -> 40.3 us (0.902)
  local copies, waits for them, and re-layouts: 2.69 us -> 0 us
  Pallas kernels: 41.2 us -> 39.6 us
    unnamed x4 -> x0, local copies, waits for them, and re-layouts: 2.69 us -> none
    pallas_call x1 -> x2, Pallas kernels: 41.2 us -> 39.6 us  [the longest x1 38.7 us: local(): pl.pallas_call(kernel, out_shape=(pltpu.VMEM((3, T, 512), BF16), pltpu.VM...]
where the time goes in v3:
time: 40.3 us; the launch traced here: 40.2 us
  Pallas kernels  39.6 us (98%)
  between operations  0.64 us (2%)
    pallas_call x1, Pallas kernels, local(): pl.pallas_call(kernel, out_shape=(pltpu.VMEM((3, T, 512), BF16), pltpu.VM...  38.7 us
    pallas_call x1, Pallas kernels, local(): pl.pallas_call(deliver, out_shape=(jax.ShapeDtypeStruct((3, T, 512), BF16...  0.9 us

profile of v3, /device:TPU:1, one launch (start us, length us, event | category | flops | bytes accessed | tf_op | source)
XLA Modules:
  0.0 40.2 jit_solution(8460489942978169761)
XLA Ops:
  0.6 38.7 %shard_map.59 = (bf16[3,256,512]{2,1,0:T(8,128)(2,1)S(1)}, f32[8,1024]{1,0:T(8,128)S(1)}) custom-call(bf16[3,256,512]{2,1,0:T(8,128)(2,1)} %bitcast.7, bf16[256,1024]{1,0:T(8,128)(2,1)} %bitcast.9, bf16[512,1024]{1,0:T(8,128)(2,1)} %w_ref.1, s32[2,8]{1,0:T(2,128)} %off_hbm.1), custom_call_target="tpu_custom_call" | custom-call | flops 1200000000 | bytes 4000000 | tf_op jit(solution)/shard_map/pallas_call | solution.py:514
  39.3 0.9 %shard_map.60 = (bf16[3,256,512]{2,1,0:T(8,128)(2,1)}, f32[8,1024]{1,0:T(8,128)}) custom-call(bf16[3,256,512]{2,1,0:T(8,128)(2,1)S(1)} %get-tuple-element.6.grads_ref, f32[8,1024]{1,0:T(8,128)S(1)} %get-tuple-element.7.weight_ref), custom_call_target="tpu_custom_call" | custom-call | tf_op jit(solution)/shard_map/pallas_call | solution.py:581

commit v4 on v3

--- a/solution.py
+++ b/solution.py
@@ -27,10 +27,10 @@
 
 def kernel(
     qkv_ref, dout_ref, w_ref, off_hbm, out_ref, wg_ref,
-    qkv_in, dout2, wv, perm, x, oth, sibs, sibr, kn, ns, kf, fs, qn, qf, g,
+    qkv_in, dout2, pdout, wv, perm, x, oth, sibs, sibr, kn, ns, kf, fs, qn, qf, g,
     o1, t1, m1, o2, t2, m2, o3, t3, m3, p1, pn, pf, attn,
     g1, q1, f1s, d1, gn, g2, q2, f2s, d2, gf, g3, q3, f3s, d3,
-    acc, nsend, nrecv, fsend, frecv, wgs, wgr, zsb, zr, off_ref,
+    acc, nsend, nrecv, fown, fsend, frecv, fback, fhome, wgs, wgr, zsb, zr, off_ref,
     load_sem, sib_s, sib_r, near_s, near_r, far_s, far_r, xy_s, xy_r, zy_s, zy_r, known,
 ):
     pos = lax.axis_index("seq")
@@ -38,14 +38,18 @@
     c = pos % 2
     xx = (pos // 2) % XS
     z = pos // (2 * XS)
-    chip = (z % 2) * XS + xx
 
     def at(z_, x_, c_):
         return (z_ * XS + x_) * 2 + c_
 
-    def far_pos(d, r):
-        ch = (chip + d + 8) % 8
-        return at(z - z % 2 + ch // XS, ch % XS, (c + r) % 2)
+    zp = z + 1 - 2 * (z % 2)
+
+    def far_pos(dz, dx, r):
+        return at(z if dz == 0 else zp, (xx + dx + XS) % XS, (c + r) % 2)
+
+    def far_peers():
+        peers = [(dz, dx, r) for dz in (1, 0) for dx in (2, 1, 3, 0) for r in (0, 1)]
+        return [peer for peer in peers if peer[:2] != (0, 0)]
 
     xp = xx + 1 - 2 * (xx % 2)
     sib = at(z, xx, 1 - c)
@@ -87,9 +91,8 @@
     tell(barrier, at(z_outer, xx, c))
     for d in range(1, YS):
         tell(barrier, pos, (y + d) % YS)
-    for d in range(7, 0, -1):
-        for r in range(2):
-            tell(barrier, far_pos(d, r))
+    for peer in far_peers():
+        tell(barrier, far_pos(*peer))
     tell(barrier, sib)
 
     lane = lax.broadcasted_iota(jnp.int32, (1, 128), 1)
@@ -147,8 +150,15 @@
         qf[p, 0] = far_rows(x[0, 0, p], far_own)
     pl.semaphore_wait(barrier, 15 + (YS - 1) + 1)
 
-    sib_copy = remote(oth, x.at[1], sib_s.at[0], sib_r.at[0], sib)
-    sib_copy.start()
+    far_copies = []
+    for dz, dx, r in far_peers():
+        slot = 8 * dz + 2 * dx + r
+        copy = remote(
+            kf.at[0] if r == 0 else fs, kf.at[slot],
+            far_s.at[0, slot], far_r.at[0, slot], far_pos(dz, dx, r),
+        )
+        copy.start()
+        far_copies.append(copy)
     near_copies = []
     for r in range(2):
         copy = remote(
@@ -156,16 +166,8 @@
         )
         copy.start()
         near_copies.append(copy)
-    far_copies = []
-    for d in range(1, 8):
-        for r in range(2):
-            slot = 2 * (d - 1) + r
-            copy = remote(
-                kf.at[0] if r == 0 else fs, kf.at[2 + slot],
-                far_s.at[0, slot], far_r.at[0, slot], far_pos(d, r),
-            )
-            copy.start()
-            far_copies.append(copy)
+    sib_copy = remote(oth, x.at[1], sib_s.at[0], sib_r.at[0], sib)
+    sib_copy.start()
     load_dout.wait()
     dout_copy = remote(dout2.at[0], dout2.at[1], sib_s.at[1], sib_r.at[1], sib)
     dout_copy.start()
@@ -201,8 +203,10 @@
         lax.fori_loop(0, 2, body, 0)
 
     def grad_in(s):
-        grads = dot_nt(dout2[s], wv[...]).astype(BF16)
-        moved = dot(perm[...], grads).astype(BF16)
+        for k in range(4):
+            columns = slice(256 * k, 256 * k + 256)
+            pdout[s, :, columns] = dot(perm[...], dout2[s, :, columns]).astype(BF16)
+        moved = dot_nt(pdout[s], wv[...]).astype(BF16)
         g[s, 0] = moved[:, :128]
         g[s, 1] = moved[:, 128:]
 
@@ -224,6 +228,21 @@
     dout_copy.wait()
     grad_in(1)
 
+    for copy in far_copies:
+        copy.wait()
+    pl.semaphore_wait(known.at[1], 2)
+    tell(known.at[2], sib)
+
+    def far_forward(p, carry):
+        out, total, peak = forward(
+            qf[p].reshape(32, 128), kf[:, 0, p].reshape(T, 128), kf[:, 1, p].reshape(T, 128),
+            pf.at[p],
+        )
+        o3[p], t3[p], m3[p] = (a.reshape(2, 16, 128) for a in (out, total, peak))
+        return carry
+
+    for p in range(2):
+        far_forward(p, 0)
     for copy in near_copies:
         copy.wait()
 
@@ -235,21 +254,8 @@
         o2[p], t2[p], m2[p] = (a.reshape(2, 64, 128) for a in (out, total, peak))
         return carry
 
-    lax.fori_loop(0, 2, near_forward, 0)
-    for copy in far_copies:
-        copy.wait()
-    pl.semaphore_wait(known.at[1], 2)
-    tell(known.at[2], sib)
-
-    def far_forward(p, carry):
-        out, total, peak = forward(
-            qf[p].reshape(32, 128), kf[:, 0, p].reshape(T, 128), kf[:, 1, p].reshape(T, 128),
-            pf.at[p],
-        )
-        o3[p], t3[p], m3[p] = (a.reshape(2, 16, 128) for a in (out, total, peak))
-        return carry
-
-    lax.fori_loop(0, 2, far_forward, 0)
+    for p in range(2):
+        near_forward(p, 0)
 
     same_head = (
         (lax.broadcasted_iota(jnp.int32, (256, 128), 0) % 128 < E)
@@ -305,27 +311,27 @@
 
     for s in range(2):
         rows = jnp.concatenate([combine(p, s) for p in range(2)], axis=1)
-        attn[s * T : (s + 1) * T, :] = dot(perm[...], rows).astype(BF16)
+        attn[s * T : (s + 1) * T, :] = rows
 
     pl.semaphore_wait(known.at[2], 1)
-    for k in range(YS):
-        columns = slice(256 * k, 256 * k + 256)
-        both = dot_tn(attn[0:T, :], dout2[0, :, columns])
-        both = both + dot_tn(attn[T:, :], dout2[1, :, columns])
+    xy_copies = []
+    for dy in (2, 1, 3, 0):
+        ty = (y + dy) % YS
+        columns = pl.ds(pl.multiple_of(256 * ty, 256), 256)
+        both = dot_tn(attn[0:T, :], pdout[0, :, columns])
+        both = both + dot_tn(attn[T:, :], pdout[1, :, columns])
         shaped = both.astype(BF16).reshape(4, XS, 16, 256)
         for to in range(XS):
-            wgs[to, k] = shaped[:, to]
-    xy_copies = []
-    for dx in range(XS):
-        for dy in range(YS):
+            wgs[dy, to] = shaped[:, to]
+        for dx in (2, 1, 3, 0):
             if dx + dy > 0:
                 slot = dx * YS + dy - 1
-                tx, ty = (xx + dx) % XS, (y + dy) % YS
+                tx = (xx + dx) % XS
                 copy = remote(
-                    wgs.at[tx, ty], wgr.at[slot], xy_s.at[slot], xy_r.at[slot], at(z, tx, c), ty
+                    wgs.at[dy, tx], wgr.at[slot], xy_s.at[slot], xy_r.at[slot], at(z, tx, c), ty
                 )
                 copy.start()
-                xy_copies.append(copy)
+                xy_copies.append((slot, copy))
 
     def backward(key, value, grads, dstat, factor, query_f, grads_f, probs_ref):
         scores = []
@@ -375,21 +381,13 @@
             acc[s, 0, p] += far_spread(grad_q[s], off)
         for k, part in enumerate((grad_k, grad_v)):
             part = part.reshape(16, 16, 128)
-            for s in range(2):
-                acc[s, 1 + k, p] += far_spread(part[s], off)
-            fsend[:, k, p] = part[2:].astype(BF16)
+            fown[:, k, p] = part[:8]
+            fsend[:, k, p] = part[8:].astype(BF16)
         return carry
 
     lax.fori_loop(0, 2, far_backward, 0)
-    far_back = []
-    for d in range(1, 8):
-        for r in range(2):
-            slot = 2 * (d - 1) + r
-            copy = remote(
-                fsend.at[slot], frecv.at[slot],
-                far_s.at[1, slot], far_r.at[1, slot], far_pos(-d, r),
-            )
-            far_back.append(copy)
+    plane_back = remote(fsend, frecv, far_s.at[1, 0], far_r.at[1, 0], at(zp, xx, c))
+    plane_back.start()
 
     def dense_backward(s):
         def body(p, carry):
@@ -398,35 +396,49 @@
                 p1.at[s, p],
             )
             for t, part in enumerate(grad_parts):
-                if s == 1:
-                    sibs[t, p] = (acc[s, t, p] + part).astype(BF16)
-                else:
-                    acc[s, t, p] += part
+                acc[s, t, p] += part
             return carry
 
         lax.fori_loop(0, 2, body, 0)
 
     dense_backward(1)
+    plane_back.wait()
+    for k in range(2):
+        for p in range(2):
+            off = offsets(1, c, p)
+            both = fown[:, k, p] + frecv[:, k, p].astype(F32)
+            for s in range(2):
+                acc[s, 1 + k, p] += far_spread(both[s], off)
+            fback[:, k, p] = both[2:].astype(BF16)
+    sibs[...] = acc[1].astype(BF16)
     sib_back = remote(sibs, sibr, sib_s.at[2], sib_r.at[2], sib)
     sib_back.start()
+    far_back = []
+    for dx in (2, 1, 3):
+        for r in range(2):
+            slot = 2 * (dx - 1) + r
+            copy = remote(
+                fback.at[slot], fhome.at[slot], far_s.at[1, 8 + slot], far_r.at[1, 8 + slot],
+                far_pos(0, -dx, r),
+            )
+            far_back.append(copy)
 
     dense_backward(0)
 
-    for copy in xy_copies:
+    for _, copy in xy_copies:
         copy.wait_send()
     for copy in near_back + far_back:
         copy.start()
-    for copy in xy_copies:
+    total = wgs[0, xx].astype(F32)
+    for slot, copy in reversed(xy_copies):
         copy.wait_recv()
-    total = wgs[xx, y].astype(F32)
-    for d in range(XS * YS - 1):
-        total = total + wgr[d].astype(F32)
+        total = total + wgr[slot].astype(F32)
     for a in range(4):
         for half in range(2):
             chunk = total[a, 8 * half : 8 * half + 8]
             zsb[a, half] = jnp.concatenate([chunk[:, :128], chunk[:, 128:]], axis=0).astype(BF16)
     zy_copies = []
-    for dy in range(YS):
+    for dy in (2, 1, 3, 0):
         for a in range(4):
             for half in range(2):
                 target = at(4 * c + a, xx, half)
@@ -456,9 +468,9 @@
     def returned(t, p, r):
         half = c if r == 0 else 1 - c
         near = near_spread(nrecv[r, t - 1, p].astype(F32), offsets(0, half, p))
-        far = frecv[r, t - 1, p].astype(F32)
-        for d in range(1, 7):
-            far = far + frecv[2 * d + r, t - 1, p].astype(F32)
+        far = fhome[r, t - 1, p].astype(F32)
+        for d in range(1, 3):
+            far = far + fhome[2 * d + r, t - 1, p].astype(F32)
         return near + far_spread(far, offsets(1, half, p))
 
     def write(t, columns, parts):
@@ -490,7 +502,6 @@
         for k in range(ZS):
             arrived = zr.at[dy, k]
             remote(arrived, arrived, zy_s.at[0, 0, 0], zy_r.at[dy, k], sib).wait_recv()
-        for k in range(ZS):
             total = total + zr[dy, k].astype(F32)
         total = total * (1.0 / YS)
         first = 256 * ((y - dy + YS) % YS)
@@ -526,7 +537,7 @@
         out_specs=(pl.BlockSpec(memory_space=pltpu.VMEM), pl.BlockSpec(memory_space=pltpu.VMEM)),
         scratch_shapes=[
             vmem((3, T, 512), BF16),
-            vmem((2, T, 1024), BF16),
+            *[vmem((2, T, 1024), BF16)] * 2,
             vmem((256, 1024), BF16),
             vmem((T, T), BF16),
             vmem((2, 3, 2, T, 128), BF16),
@@ -556,8 +567,9 @@
             vmem((2, 3, 2, T, 128), F32),
             vmem((2, 2, 2, 64, 128), BF16),
             vmem((2, 2, 2, 64, 128), BF16),
-            vmem((14, 2, 2, 16, 128), BF16),
-            vmem((14, 2, 2, 16, 128), BF16),
+            vmem((8, 2, 2, 16, 128), F32),
+            *[vmem((8, 2, 2, 16, 128), BF16)] * 2,
+            *[vmem((6, 2, 2, 16, 128), BF16)] * 2,
             vmem((4, 4, 4, 16, 256), BF16),
             vmem((15, 4, 16, 256), BF16),
             vmem((4, 2, 16, 128), BF16),
@@ -566,7 +578,7 @@
             dma((4,)),
             dma((3,)), dma((3,)),
             dma((2, 2)), dma((2, 2)),
-            dma((2, 14)), dma((2, 14)),
+            dma((2, 16)), dma((2, 16)),
             dma((15,)), dma((15,)),
             dma((4, 4, 2)), dma((4, 8)),
             pltpu.SemaphoreType.REGULAR((3,)),

time: 40.3 us -> 37.7 us (0.935)
  Pallas kernels: 39.6 us -> 36.9 us
    pallas_call x1, Pallas kernels: 38.7 us -> 36 us  [local(): pl.pallas_call(kernel, out_shape=(pltpu.VMEM((3, T, 512), BF16), pltpu.VM...]
where the time goes in v4:
time: 37.7 us; the launch traced here: 37.6 us
  Pallas kernels  36.9 us (98%)
  between operations  0.64 us (2%)
    pallas_call x1, Pallas kernels, local(): pl.pallas_call(kernel, out_shape=(pltpu.VMEM((3, T, 512), BF16), pltpu.VM...  36 us
    pallas_call x1, Pallas kernels, local(): pl.pallas_call(deliver, out_shape=(jax.ShapeDtypeStruct((3, T, 512), BF16...  0.9 us

profile of v4, /device:TPU:1, one launch (start us, length us, event | category | flops | bytes accessed | tf_op | source)
XLA Modules:
  0.0 37.6 jit_solution(10531338576728868567)
XLA Ops:
  0.6 36.0 %shard_map.59 = (bf16[3,256,512]{2,1,0:T(8,128)(2,1)S(1)}, f32[8,1024]{1,0:T(8,128)S(1)}) custom-call(bf16[3,256,512]{2,1,0:T(8,128)(2,1)} %bitcast.7, bf16[256,1024]{1,0:T(8,128)(2,1)} %bitcast.9, bf16[512,1024]{1,0:T(8,128)(2,1)} %w_ref.1, s32[2,8]{1,0:T(2,128)} %off_hbm.1), custom_call_target="tpu_custom_call" | custom-call | flops 1200000000 | bytes 4000000 | tf_op jit(solution)/shard_map/pallas_call | solution.py:525
  36.7 0.9 %shard_map.60 = (bf16[3,256,512]{2,1,0:T(8,128)(2,1)}, f32[8,1024]{1,0:T(8,128)}) custom-call(bf16[3,256,512]{2,1,0:T(8,128)(2,1)S(1)} %get-tuple-element.6.grads_ref, f32[8,1024]{1,0:T(8,128)S(1)} %get-tuple-element.7.weight_ref), custom_call_target="tpu_custom_call" | custom-call | tf_op jit(solution)/shard_map/pallas_call | solution.py:593

commit v5 on v4

--- a/solution.py
+++ b/solution.py
@@ -200,7 +200,8 @@
             o1[s, p], t1[s, p], m1[s, p] = out, total, peak
             return carry
 
-        lax.fori_loop(0, 2, body, 0)
+        for p in range(2):
+            body(p, 0)
 
     def grad_in(s):
         for k in range(4):
@@ -310,28 +311,25 @@
         return low
 
     for s in range(2):
-        rows = jnp.concatenate([combine(p, s) for p in range(2)], axis=1)
-        attn[s * T : (s + 1) * T, :] = rows
+        for p in range(2):
+            attn[128 * p : 128 * p + 128, s * T : (s + 1) * T] = jnp.transpose(combine(p, s))
 
     pl.semaphore_wait(known.at[2], 1)
     xy_copies = []
     for dy in (2, 1, 3, 0):
         ty = (y + dy) % YS
         columns = pl.ds(pl.multiple_of(256 * ty, 256), 256)
-        both = dot_tn(attn[0:T, :], pdout[0, :, columns])
-        both = both + dot_tn(attn[T:, :], pdout[1, :, columns])
+        both = dot(attn[...], pdout[:, :, columns].reshape(2 * T, 256))
         shaped = both.astype(BF16).reshape(4, XS, 16, 256)
         for to in range(XS):
             wgs[dy, to] = shaped[:, to]
-        for dx in (2, 1, 3, 0):
-            if dx + dy > 0:
-                slot = dx * YS + dy - 1
-                tx = (xx + dx) % XS
-                copy = remote(
-                    wgs.at[dy, tx], wgr.at[slot], xy_s.at[slot], xy_r.at[slot], at(z, tx, c), ty
-                )
-                copy.start()
-                xy_copies.append((slot, copy))
+    for dx, dy in ((2, 2), (2, 1), (2, 3), (1, 2), (3, 2), (2, 0), (0, 2), (1, 1), (1, 3), (3, 1),
+                   (3, 3), (1, 0), (3, 0), (0, 1), (0, 3)):
+        slot = dx * YS + dy - 1
+        tx, ty = (xx + dx) % XS, (y + dy) % YS
+        copy = remote(wgs.at[dy, tx], wgr.at[slot], xy_s.at[slot], xy_r.at[slot], at(z, tx, c), ty)
+        copy.start()
+        xy_copies.append((slot, copy))
 
     def backward(key, value, grads, dstat, factor, query_f, grads_f, probs_ref):
         scores = []
@@ -364,7 +362,8 @@
                 nsend[r, k, p] = part[2 + r].astype(BF16)
         return carry
 
-    lax.fori_loop(0, 2, near_backward, 0)
+    for p in range(2):
+        near_backward(p, 0)
     near_back = []
     for r in range(2):
         copy = remote(nsend.at[r], nrecv.at[r], near_s.at[1, r], near_r.at[1, r], near_pos(r))
@@ -385,7 +384,8 @@
             fsend[:, k, p] = part[8:].astype(BF16)
         return carry
 
-    lax.fori_loop(0, 2, far_backward, 0)
+    for p in range(2):
+        far_backward(p, 0)
     plane_back = remote(fsend, frecv, far_s.at[1, 0], far_r.at[1, 0], at(zp, xx, c))
     plane_back.start()
 
@@ -399,7 +399,8 @@
                 acc[s, t, p] += part
             return carry
 
-        lax.fori_loop(0, 2, body, 0)
+        for p in range(2):
+            body(p, 0)
 
     dense_backward(1)
     plane_back.wait()
@@ -557,7 +558,7 @@
             vmem((2, 2, 2, T, T), BF16),
             vmem((2, 2, 128, T), BF16),
             vmem((2, 2, 32, T), BF16),
-            vmem((2 * T, 256), BF16),
+            vmem((256, 2 * T), BF16),
             *[vmem((2, 2, T, 128), BF16)] * 2,
             *[vmem((2, 2, T, 128), F32)] * 2,
             *[vmem((2, 2, 64, 128), BF16)] * 3,

time: 37.7 us -> 36.9 us (0.979)
  Pallas kernels: 36.9 us -> 36.1 us
    pallas_call x1, Pallas kernels: 36 us -> 35.2 us  [local(): pl.pallas_call(kernel, out_shape=(pltpu.VMEM((3, T, 512), BF16), pltpu.VM...]
where the time goes in v5:
time: 36.9 us; the launch traced here: 36.8 us
  Pallas kernels  36.1 us (98%)
  between operations  0.64 us (2%)
    pallas_call x1, Pallas kernels, local(): pl.pallas_call(kernel, out_shape=(pltpu.VMEM((3, T, 512), BF16), pltpu.VM...  35.2 us
    pallas_call x1, Pallas kernels, local(): pl.pallas_call(deliver, out_shape=(jax.ShapeDtypeStruct((3, T, 512), BF16...  0.9 us

profile of v5, /device:TPU:1, one launch (start us, length us, event | category | flops | bytes accessed | tf_op | source)
XLA Modules:
  0.0 36.8 jit_solution(9463426922243386533)
XLA Ops:
  0.6 35.2 %shard_map.59 = (bf16[3,256,512]{2,1,0:T(8,128)(2,1)S(1)}, f32[8,1024]{1,0:T(8,128)S(1)}) custom-call(bf16[3,256,512]{2,1,0:T(8,128)(2,1)} %bitcast.7, bf16[256,1024]{1,0:T(8,128)(2,1)} %bitcast.9, bf16[512,1024]{1,0:T(8,128)(2,1)} %w_ref.1, s32[2,8]{1,0:T(2,128)} %off_hbm.1), custom_call_target="tpu_custom_call" | custom-call | flops 1200000000 | bytes 4000000 | tf_op jit(solution)/shard_map/pallas_call | solution.py:526
  35.9 0.9 %shard_map.60 = (bf16[3,256,512]{2,1,0:T(8,128)(2,1)}, f32[8,1024]{1,0:T(8,128)}) custom-call(bf16[3,256,512]{2,1,0:T(8,128)(2,1)S(1)} %get-tuple-element.6.grads_ref, f32[8,1024]{1,0:T(8,128)S(1)} %get-tuple-element.7.weight_ref), custom_call_target="tpu_custom_call" | custom-call | tf_op jit(solution)/shard_map/pallas_call | solution.py:594

commit v6 on v5

--- a/solution.py
+++ b/solution.py
@@ -29,7 +29,7 @@
     qkv_ref, dout_ref, w_ref, off_hbm, out_ref, wg_ref,
     qkv_in, dout2, pdout, wv, perm, x, oth, sibs, sibr, kn, ns, kf, fs, qn, qf, g,
     o1, t1, m1, o2, t2, m2, o3, t3, m3, p1, pn, pf, attn,
-    g1, q1, f1s, d1, gn, g2, q2, f2s, d2, gf, g3, q3, f3s, d3,
+    lows, f2w, f3w, g1, q1, f1s, d1, gn, g2, q2, f2s, d2, gf, g3, q3, f3s, d3,
     acc, nsend, nrecv, fown, fsend, frecv, fback, fhome, wgs, wgr, zsb, zr, off_ref,
     load_sem, sib_s, sib_r, near_s, near_r, far_s, far_r, xy_s, xy_r, zy_s, zy_r, known,
 ):
@@ -207,12 +207,13 @@
         for k in range(4):
             columns = slice(256 * k, 256 * k + 256)
             pdout[s, :, columns] = dot(perm[...], dout2[s, :, columns]).astype(BF16)
+
+    def grad_attn(s):
         moved = dot_nt(pdout[s], wv[...]).astype(BF16)
         g[s, 0] = moved[:, :128]
         g[s, 1] = moved[:, 128:]
 
     dense_forward(0)
-    load_w.wait()
     grad_in(0)
     sib_copy.wait()
     for p in range(2):
@@ -286,28 +287,8 @@
         f1, f2, f3 = e1 * inverse, e2 * inverse, e3 * inverse
         mixed = f1 * o1[s, p] + f2 * near_wide(o2[p, s]) + f3 * far_wide(o3[p, s])
         low = mixed.astype(BF16)
-        grads = g[s, p].astype(F32)
-        query = x[s, 0, p].astype(F32)
-        product = grads * low.astype(F32)
-        high = product.astype(BF16)
-        rest = (product - high.astype(F32)).astype(BF16)
-        dstat = dot(jnp.concatenate([high, rest], axis=1), same_head)
-        g1[s, p] = (grads * f1).astype(BF16)
-        q1[s, p] = (query * f1).astype(BF16)
-        f1s[s, p] = f1
-        d1[s, p] = dstat
-        near_f, near_g = near_rows(f2, near_off), near_rows(g[s, p], near_off)
-        gn[p, s] = near_g
-        g2[p, s] = (near_g.astype(F32) * near_f).astype(BF16)
-        q2[p, s] = (qn[p, s].astype(F32) * near_f).astype(BF16)
-        f2s[p, s] = near_f
-        d2[p, s] = near_rows(dstat, near_off)
-        far_f, far_g = far_rows(f3, far_off), far_rows(g[s, p], far_off)
-        gf[p, s] = far_g
-        g3[p, s] = (far_g.astype(F32) * far_f).astype(BF16)
-        q3[p, s] = (qf[p, s].astype(F32) * far_f).astype(BF16)
-        f3s[p, s] = far_f
-        d3[p, s] = far_rows(dstat, far_off)
+        lows[s, p] = low
+        f1s[s, p], f2w[s, p], f3w[s, p] = f1, f2, f3
         return low
 
     for s in range(2):
@@ -330,6 +311,37 @@
         copy = remote(wgs.at[dy, tx], wgr.at[slot], xy_s.at[slot], xy_r.at[slot], at(z, tx, c), ty)
         copy.start()
         xy_copies.append((slot, copy))
+
+    def prepare(p, s):
+        near_off, far_off = offsets(0, c, p), offsets(1, c, p)
+        low, f1, f2, f3 = lows[s, p], f1s[s, p], f2w[s, p], f3w[s, p]
+        grads = g[s, p].astype(F32)
+        query = x[s, 0, p].astype(F32)
+        product = grads * low.astype(F32)
+        high = product.astype(BF16)
+        rest = (product - high.astype(F32)).astype(BF16)
+        dstat = dot(jnp.concatenate([high, rest], axis=1), same_head)
+        g1[s, p] = (grads * f1).astype(BF16)
+        q1[s, p] = (query * f1).astype(BF16)
+        d1[s, p] = dstat
+        near_f, near_g = near_rows(f2, near_off), near_rows(g[s, p], near_off)
+        gn[p, s] = near_g
+        g2[p, s] = (near_g.astype(F32) * near_f).astype(BF16)
+        q2[p, s] = (qn[p, s].astype(F32) * near_f).astype(BF16)
+        f2s[p, s] = near_f
+        d2[p, s] = near_rows(dstat, near_off)
+        far_f, far_g = far_rows(f3, far_off), far_rows(g[s, p], far_off)
+        gf[p, s] = far_g
+        g3[p, s] = (far_g.astype(F32) * far_f).astype(BF16)
+        q3[p, s] = (qf[p, s].astype(F32) * far_f).astype(BF16)
+        f3s[p, s] = far_f
+        d3[p, s] = far_rows(dstat, far_off)
+
+    load_w.wait()
+    for s in range(2):
+        grad_attn(s)
+        for p in range(2):
+            prepare(p, s)
 
     def backward(key, value, grads, dstat, factor, query_f, grads_f, probs_ref):
         scores = []
@@ -559,6 +571,8 @@
             vmem((2, 2, 128, T), BF16),
             vmem((2, 2, 32, T), BF16),
             vmem((256, 2 * T), BF16),
+            vmem((2, 2, T, 128), BF16),
+            *[vmem((2, 2, T, 128), F32)] * 2,
             *[vmem((2, 2, T, 128), BF16)] * 2,
             *[vmem((2, 2, T, 128), F32)] * 2,
             *[vmem((2, 2, 64, 128), BF16)] * 3,

time: 36.9 us -> 36.5 us (0.989)
  no operation moved by 1% of the time
where the time goes in v6:
time: 36.5 us; the launch traced here: 36.4 us
  Pallas kernels  35.8 us (98%)
  between operations  0.64 us (2%)
    pallas_call x1, Pallas kernels, local(): pl.pallas_call(kernel, out_shape=(pltpu.VMEM((3, T, 512), BF16), pltpu.VM...  34.9 us
    pallas_call x1, Pallas kernels, local(): pl.pallas_call(deliver, out_shape=(jax.ShapeDtypeStruct((3, T, 512), BF16...  0.9 us

profile of v6, /device:TPU:1, one launch (start us, length us, event | category | flops | bytes accessed | tf_op | source)
XLA Modules:
  0.0 36.4 jit_solution(1002845572565998206)
XLA Ops:
  0.6 34.9 %shard_map.59 = (bf16[3,256,512]{2,1,0:T(8,128)(2,1)S(1)}, f32[8,1024]{1,0:T(8,128)S(1)}) custom-call(bf16[3,256,512]{2,1,0:T(8,128)(2,1)} %bitcast.7, bf16[256,1024]{1,0:T(8,128)(2,1)} %bitcast.9, bf16[512,1024]{1,0:T(8,128)(2,1)} %w_ref.1, s32[2,8]{1,0:T(2,128)} %off_hbm.1), custom_call_target="tpu_custom_call" | custom-call | flops 1200000000 | bytes 4000000 | tf_op jit(solution)/shard_map/pallas_call | solution.py:538
  35.5 0.9 %shard_map.60 = (bf16[3,256,512]{2,1,0:T(8,128)(2,1)}, f32[8,1024]{1,0:T(8,128)}) custom-call(bf16[3,256,512]{2,1,0:T(8,128)(2,1)S(1)} %get-tuple-element.6.grads_ref, f32[8,1024]{1,0:T(8,128)S(1)} %get-tuple-element.7.weight_ref), custom_call_target="tpu_custom_call" | custom-call | tf_op jit(solution)/shard_map/pallas_call | solution.py:608

commit v7 on v6

--- a/solution.py
+++ b/solution.py
@@ -214,7 +214,6 @@
         g[s, 1] = moved[:, 128:]
 
     dense_forward(0)
-    grad_in(0)
     sib_copy.wait()
     for p in range(2):
         near_own, far_own = offsets(0, c, p), offsets(1, c, p)
@@ -227,8 +226,6 @@
     pl.semaphore_wait(known.at[0], 2)
     for d in (-2, 2):
         tell(known.at[1], z_pos(d))
-    dout_copy.wait()
-    grad_in(1)
 
     for copy in far_copies:
         copy.wait()
@@ -245,6 +242,9 @@
 
     for p in range(2):
         far_forward(p, 0)
+    grad_in(0)
+    dout_copy.wait()
+    grad_in(1)
     for copy in near_copies:
         copy.wait()
 

time: 36.5 us -> 36.6 us (level)
  no operation moved by 1% of the time
where the time goes in v7:
time: 36.6 us; the launch traced here: 36.5 us
  Pallas kernels  35.8 us (98%)
  between operations  0.64 us (2%)
    pallas_call x1, Pallas kernels, local(): pl.pallas_call(kernel, out_shape=(pltpu.VMEM((3, T, 512), BF16), pltpu.VM...  34.9 us
    pallas_call x1, Pallas kernels, local(): pl.pallas_call(deliver, out_shape=(jax.ShapeDtypeStruct((3, T, 512), BF16...  0.9 us

profile of v7, /device:TPU:1, one launch (start us, length us, event | category | flops | bytes accessed | tf_op | source)
XLA Modules:
  0.0 36.5 jit_solution(6636179709974860826)
XLA Ops:
  0.6 34.9 %shard_map.59 = (bf16[3,256,512]{2,1,0:T(8,128)(2,1)S(1)}, f32[8,1024]{1,0:T(8,128)S(1)}) custom-call(bf16[3,256,512]{2,1,0:T(8,128)(2,1)} %bitcast.7, bf16[256,1024]{1,0:T(8,128)(2,1)} %bitcast.9, bf16[512,1024]{1,0:T(8,128)(2,1)} %w_ref.1, s32[2,8]{1,0:T(2,128)} %off_hbm.1), custom_call_target="tpu_custom_call" | custom-call | flops 1200000000 | bytes 4000000 | tf_op jit(solution)/shard_map/pallas_call | solution.py:538
  35.6 0.9 %shard_map.60 = (bf16[3,256,512]{2,1,0:T(8,128)(2,1)}, f32[8,1024]{1,0:T(8,128)}) custom-call(bf16[3,256,512]{2,1,0:T(8,128)(2,1)S(1)} %get-tuple-element.6.grads_ref, f32[8,1024]{1,0:T(8,128)S(1)} %get-tuple-element.7.weight_ref), custom_call_target="tpu_custom_call" | custom-call | tf_op jit(solution)/shard_map/pallas_call | solution.py:608
